TPU v7x, 512 devices: a whole 4x4x16 slice. The times are simulated.
512 devices in a mesh: region: 2 (over x_lo), sector: 32 (over z, core), block: 8 (over x_hi, y).
Axes of the slice: x: 4 (x_hi: 2, x_lo: 2; x = x_hi * 2 + x_lo), y: 4, z: 16, core: 2. Of those that a mesh axis runs over, the one named last changes fastest.
Arguments:
- number_concentration: float32 [2, 64, 16, 256, 128], P('region', None, 'block', 'sector'), may hold values from 0.05 to 2
- frame_motion_vector: float32 [2, 3, 16, 256, 128], P('region', None, 'block', 'sector'), may hold values from -1 to 1
- strain_factor: float32 [2, 16, 256, 128], P('region', 'block', 'sector'), may hold values from 0.1 to 1
- splitting_kernel: float32 [64, 64], replicated, may hold values from -0.75 to 0.75
- merging_kernel: float32 [64, 64], replicated, may hold values from -0.75 to 0.75
- spinning_shift_history: int32 [2], replicated, may hold values from 0 to 255
- nearest_coverage_fraction: float32 [2], replicated, may hold values from 0.05 to 0.95
Outputs:
- evolved: float32 [2, 64, 16, 256, 128], P('region', None, 'block', 'sector')
All inputs are finite; a program needn't handle non-finite values.
Results may differ from a plain program's by a relative error of at most 0.0001.
Values sent between devices are 32-bit elements; how exact they have to be, the bound alone decides.
No kernel may reach another device: no remote copies, remote signals or barrier semaphores. Data moves between devices by JAX's collectives and lax.ppermute only.
A program may use at most 64 MiB of HBM per device.

v0:
```python
import functools

import jax
import jax.numpy as jnp
from jax import lax
from jax.experimental import pallas as pl
from jax.experimental.pallas import tpu as pltpu
from jax.sharding import PartitionSpec as P

TIME_STEP = 0.2
AXES = ("region", "sector", "block")
SECTIONS = 64
CELLS = 8
ROWS = 2
AXIAL = 128
ROW_BYTES_ROWS = CELLS * SECTIONS
STRIDE = ROWS * CELLS
OWN = 40
CROSS = SECTIONS - OWN
DIRECT_CHIPS = 1
EDGE = ROW_BYTES_ROWS + SECTIONS


def device_number(region, sector, block):
    return (region * lax.axis_size("sector") + sector) * lax.axis_size("block") + block


def sector_pairs(step):
    count = lax.axis_size("sector")
    return [
        (device_number(r, s, b), device_number(r, (s + step) % count, b))
        for r in range(2)
        for s in range(count)
        for b in range(lax.axis_size("block"))
    ]


def block_pairs(step):
    count = lax.axis_size("block")
    return [
        (device_number(r, s, b), device_number(r, s, b + step))
        for r in range(2)
        for s in range(lax.axis_size("sector"))
        for b in range(count)
        if 0 <= b + step < count
    ]


def turn_pairs(sectors, across):
    count = lax.axis_size("sector")
    last = lax.axis_size("block") - 1
    return [
        (
            device_number(r, s, last),
            device_number(1 - r if across else r, (s + (sectors if (r == 0) == across else -sectors)) % count, last),
        )
        for r in range(2)
        for s in range(count)
    ]


def line(index):
    return pl.ds(index * SECTIONS, SECTIONS)


def pack_kernel(field_ref, speed_ref, up_ref, down_ref, next_ref, prev_ref):
    for row, out_ref in ((0, down_ref), (1, up_ref)):
        for a in range(CELLS):
            cells = field_ref[pl.ds(row * CELLS + a, SECTIONS, stride=STRIDE), :]
            store_cells(row, a, cells, up_ref, down_ref, next_ref, prev_ref)
        out_ref[pl.ds(ROW_BYTES_ROWS, CELLS), :] = speed_ref[pl.ds(STRIDE + row * CELLS, CELLS), :]
    for edge_ref, a in ((prev_ref, 0), (next_ref, CELLS - 1)):
        edge_ref[pl.ds(EDGE, 8), :] = jnp.zeros((8, AXIAL), jnp.float32)
        for row in range(ROWS):
            edge_ref[pl.ds(EDGE + row, 1), :] = speed_ref[pl.ds(row * CELLS + a, 1), :]


def store_cells(row, a, cells, up_ref, down_ref, next_ref, prev_ref):
    if row == ROWS - 1:
        for out_ref in (up_ref, next_ref, prev_ref):
            out_ref[line(a), :] = cells
    else:
        down_ref[line(a), :] = cells
        if a == 0:
            prev_ref[line(CELLS), :] = cells
        if a == CELLS - 1:
            next_ref[line(CELLS), :] = cells


def lines(count):
    return jax.ShapeDtypeStruct((count, AXIAL), jnp.float32)


def vmem(count):
    return [pl.BlockSpec(memory_space=pltpu.VMEM)] * count


def pack(field, speeds):
    rim = lines(ROW_BYTES_ROWS + CELLS)
    edge = lines(EDGE + 8)
    return pl.pallas_call(
        pack_kernel,
        out_shape=(rim, rim, edge, edge),
        in_specs=vmem(2),
        out_specs=tuple(vmem(4)),
        name="pack",
    )(field, speeds)


def align_kernel(substep, shift_ref, weight_ref, own_ref, prev_ref, next_ref, direct_ref, cross_ref, row_ref):
    @pl.when(lax.axis_index("block") == lax.axis_size("block") - 1)
    def _():
        on_stator = lax.axis_index("region") == 1
        residual = (shift_ref[substep] + CELLS) % STRIDE - CELLS
        weight = weight_ref[substep]
        for place, part_ref in enumerate((prev_ref, own_ref, next_ref)):
            row_ref[pl.ds(place * ROW_BYTES_ROWS, ROW_BYTES_ROWS), :] = part_ref[pl.ds(0, ROW_BYTES_ROWS), :]
        first = CELLS + jnp.where(on_stator, residual, -residual - 1)
        later_weight = jnp.where(on_stator, 1.0 - weight, weight)

        def cell(index):
            return row_ref[pl.ds(pl.multiple_of((first + index) * SECTIONS, SECTIONS), SECTIONS), :]

        for a in range(CELLS):
            ghost = later_weight * cell(a + 1) + (1.0 - later_weight) * cell(a)
            direct_ref[pl.ds(a * OWN, OWN), :] = ghost[:OWN]
            cross_ref[pl.ds(a * CROSS, CROSS), :] = ghost[OWN:]


def align(substep, shifts, weights, own, from_prev, from_next):
    return pl.pallas_call(
        functools.partial(align_kernel, substep),
        out_shape=(lines(CELLS * OWN), lines(CELLS * CROSS)),
        in_specs=[pl.BlockSpec(memory_space=pltpu.SMEM)] * 2 + vmem(3),
        out_specs=tuple(vmem(2)),
        scratch_shapes=[pltpu.VMEM((3 * ROW_BYTES_ROWS, AXIAL), jnp.float32)],
        name="align",
    )(shifts, weights, own, from_prev, from_next)


def split_halves(value):
    high = value.astype(jnp.bfloat16)
    low = (value - high.astype(jnp.float32)).astype(jnp.bfloat16)
    return high, low


def substep_kernel(
    final,
    up_ref,
    down_ref,
    prev_ref,
    next_ref,
    below_ref,
    above_ref,
    direct_ref,
    cross_ref,
    prev_rim_ref,
    next_rim_ref,
    below_rim_ref,
    above_rim_ref,
    speed_ref,
    strain_ref,
    split_ref,
    merge_ref,
    *refs,
):
    if final:
        out_ref, coef_ref, top_ref = refs
    else:
        *new_refs, coef_ref, top_ref = refs
    block = lax.axis_index("block")
    first_block = block == 0
    last_block = block == lax.axis_size("block") - 1
    below_speed = below_rim_ref[pl.ds(ROW_BYTES_ROWS, CELLS), :]
    above_speed = above_rim_ref[pl.ds(ROW_BYTES_ROWS, CELLS), :]

    @pl.when(last_block)
    def _():
        for a in range(CELLS):
            top_ref[pl.ds(a * SECTIONS, OWN), :] = direct_ref[pl.ds(a * OWN, OWN), :]
            top_ref[pl.ds(a * SECTIONS + OWN, CROSS), :] = cross_ref[pl.ds(a * CROSS, CROSS), :]

    @pl.when(jnp.logical_not(last_block))
    def _():
        top_ref[...] = above_ref[pl.ds(0, ROW_BYTES_ROWS), :]

    for row in range(ROWS):
        azim = speed_ref[pl.ds(row * CELLS, CELLS), :]
        azim_next = jnp.concatenate([azim[1:], next_rim_ref[pl.ds(EDGE + row, 1), :]], axis=0)
        azim_prev = jnp.concatenate([prev_rim_ref[pl.ds(EDGE + row, 1), :], azim[:-1]], axis=0)
        azim_high = 0.5 * (azim + azim_next)
        azim_low = 0.5 * (azim_prev + azim)
        radial = speed_ref[pl.ds(STRIDE + row * CELLS, CELLS), :]
        if row == 0:
            other = speed_ref[pl.ds(STRIDE + CELLS, CELLS), :]
            radial_high = 0.5 * (radial + other)
            radial_low = jnp.where(first_block, 0.0, 0.5 * (below_speed + radial))
        else:
            other = speed_ref[pl.ds(STRIDE, CELLS), :]
            radial_high = jnp.where(last_block, radial, 0.5 * (radial + above_speed))
            radial_low = 0.5 * (other + radial)
        axial = speed_ref[pl.ds(2 * STRIDE + row * CELLS, CELLS), :]
        axial_high = 0.5 * (axial + pltpu.roll(axial, AXIAL - 1, 1))
        axial_low = pltpu.roll(axial_high, 1, 1)
        own = 0.0
        place = row * CELLS
        for number, (high, low) in enumerate(
            ((radial_high, radial_low), (azim_high, azim_low), (axial_high, axial_low))
        ):
            own = own + jnp.maximum(high, 0.0) - jnp.minimum(low, 0.0)
            coef_ref[2 * number, pl.ds(place, CELLS), :] = -TIME_STEP * jnp.minimum(high, 0.0)
            coef_ref[2 * number + 1, pl.ds(place, CELLS), :] = TIME_STEP * jnp.maximum(low, 0.0)
        coef_ref[6, pl.ds(place, CELLS), :] = 1.0 - TIME_STEP * own
        coef_ref[7, pl.ds(place, CELLS), :] = TIME_STEP * strain_ref[pl.ds(place, CELLS), :]

    split_high, split_low = split_halves(split_ref[...])
    merge_high, merge_low = split_halves(TIME_STEP * merge_ref[...])
    both_high = jnp.concatenate([split_high, merge_high], axis=0)
    both_low = jnp.concatenate([split_low, merge_low], axis=0)
    left = jnp.concatenate([both_high, both_high, both_low], axis=1)

    for row in range(ROWS):
        own_ref = (down_ref, up_ref)[row]
        for pair in range(CELLS // 2):
            cells_of = [own_ref[line(2 * pair + i), :] for i in range(2)]
            wide = jnp.concatenate(cells_of, axis=1)
            high, low = split_halves(wide)
            right = jnp.concatenate([high, low, high], axis=0)
            products = jnp.dot(left, right, preferred_element_type=jnp.float32)
            for i in range(2):
                a = 2 * pair + i
                cells = cells_of[i]
                broken = products[:SECTIONS, i * AXIAL : (i + 1) * AXIAL]
                joined = products[SECTIONS:, i * AXIAL : (i + 1) * AXIAL]
                coef = lambda n: coef_ref[n, pl.ds(row * CELLS + a, 1), :]
                if row == 0:
                    outer, inner = up_ref[line(a), :], below_ref[line(a), :]
                else:
                    outer, inner = top_ref[line(a), :], down_ref[line(a), :]
                later = next_ref[line(0 if row else CELLS), :] if a == CELLS - 1 else own_ref[line(a + 1), :]
                earlier = prev_ref[line(CELLS - 1 if row else CELLS), :] if a == 0 else own_ref[line(a - 1), :]
                value = cells * (coef(6) + joined)
                value = value + coef(7) * broken
                value = value + (coef(0) * outer + coef(1) * inner)
                value = value + (coef(2) * later + coef(3) * earlier)
                value = value + (
                    coef(4) * pltpu.roll(cells, AXIAL - 1, 1) + coef(5) * pltpu.roll(cells, 1, 1)
                )
                if final:
                    out_ref[pl.ds(row * CELLS + a, SECTIONS, stride=STRIDE), :] = value
                else:
                    store_cells(row, a, value, *new_refs)


def run_substep(final, *arrays):
    if final:
        out_shape, out_specs = lines(SECTIONS * STRIDE), vmem(1)[0]
    else:
        out_shape = (lines(ROW_BYTES_ROWS), lines(ROW_BYTES_ROWS), lines(EDGE), lines(EDGE))
        out_specs = tuple(vmem(4))
    return pl.pallas_call(
        functools.partial(substep_kernel, final),
        out_shape=out_shape,
        in_specs=vmem(len(arrays)),
        out_specs=out_specs,
        scratch_shapes=[
            pltpu.VMEM((8, STRIDE, AXIAL), jnp.float32),
            pltpu.VMEM((ROW_BYTES_ROWS, AXIAL), jnp.float32),
        ],
        compiler_params=pltpu.CompilerParams(vmem_limit_bytes=32 * 1024 * 1024),
        name="substep",
    )(*arrays)


def turned(shift, direct, cross):
    count = lax.axis_size("sector") // 2

    def turn(chips, direct, cross):
        chips = chips % count
        distance = min(chips, count - chips)
        if distance <= DIRECT_CHIPS or 2 * distance == count:
            cross = lax.ppermute(cross, AXES, turn_pairs(2 * chips, True))
            direct = lax.ppermute(direct, AXES, turn_pairs(2 * chips, True))
        else:
            cross = lax.ppermute(cross, AXES, turn_pairs(0, True))
            direct = lax.ppermute(direct, AXES, turn_pairs(2 * chips, True))
            cross = lax.ppermute(cross, AXES, turn_pairs(2 * chips, False))
        return direct, cross

    def choose(low, high, direct, cross):
        if high - low == 1:
            return turn(low, direct, cross)
        middle = (low + high) // 2
        return lax.cond(
            shift < middle * STRIDE - CELLS,
            functools.partial(choose, low, middle),
            functools.partial(choose, middle, high),
            direct,
            cross,
        )

    return choose(0, count + 1, direct, cross)


def body(
    number_concentration,
    frame_motion_vector,
    strain_factor,
    splitting_kernel,
    merging_kernel,
    spinning_shift_history,
    nearest_coverage_fraction,
):
    field = number_concentration.reshape(SECTIONS * STRIDE, AXIAL)
    speeds = frame_motion_vector.reshape(3 * STRIDE, AXIAL)
    strain = strain_factor.reshape(STRIDE, AXIAL)
    shifts, weights = spinning_shift_history, nearest_coverage_fraction
    arrays = pack(field, speeds)
    rims = None
    for substep in range(2):
        up, down, to_next, to_prev = arrays
        from_prev = lax.ppermute(to_next, AXES, sector_pairs(1))
        from_next = lax.ppermute(to_prev, AXES, sector_pairs(-1))
        below = lax.ppermute(up, AXES, block_pairs(1))
        above = lax.ppermute(down, AXES, block_pairs(-1))
        direct, cross = align(substep, shifts, weights, up, from_prev, from_next)
        direct, cross = turned(shifts[substep], direct, cross)
        halos = (from_prev, from_next, below, above)
        rims = rims or halos
        arrays = run_substep(
            substep == 1,
            up,
            down,
            *halos,
            direct,
            cross,
            *rims,
            speeds,
            strain,
            splitting_kernel,
            merging_kernel,
        )
    return arrays.reshape(number_concentration.shape)


def solution(mesh):
    return jax.shard_map(
        body,
        mesh=mesh,
        in_specs=(
            P("region", None, "block", "sector", None),
            P("region", None, "block", "sector", None),
            P("region", "block", "sector", None),
            P(),
            P(),
            P(),
            P(),
        ),
        out_specs=P("region", None, "block", "sector", None),
        check_vma=False,
    )
```

profile of v0, /device:TPU:30, one launch (start us, length us, event | category | flops | bytes accessed | tf_op | source)
XLA Modules:
  0.0 110.8 jit_solution(4492079424066989742)
XLA Ops:
  0.0 2.1 %pack.1 = (f32[520,128]{1,0:T(8,128)}, f32[520,128]{1,0:T(8,128)}, f32[584,128]{1,0:T(8,128)}, f32[584,128]{1,0:T(8,128)}) custom-call(f32[1024,128]{1,0:T(8,128)} %bitcast.11, f32[48,128]{1,0:T(8,128)} %bitcast.6), custom_call_target="tpu_custom_call" | custom-call | tf_op jit(solution)/shard_map/pack/pallas_call | solution.py:101
  2.1 8.9 %collective-permute-start.93 = (f32[584,128]{1,0:T(8,128)}, f32[584,128]{1,0:T(8,128)S(1)}, u32[]{:S(2)}, u32[]{:S(2)}) collective-permute-start(f32[584,128]{1,0:T(8,128)} %get-tuple-element.474), channel_id=1, source_target_pairs={{0,248},{1,249},{2,250},{3,251},{4,252},{5,253},{6,254},{7,255},{8... | collective-permute-start | bytes 897032 | tf_op jit(solution)/shard_map/ppermute | solution.py:323
  11.1 1.4 %collective-permute-start.94 = (f32[520,128]{1,0:T(8,128)}, f32[520,128]{1,0:T(8,128)S(1)}, u32[]{:S(2)}, u32[]{:S(2)}) collective-permute-start(f32[520,128]{1,0:T(8,128)} %get-tuple-element.471.own_ref.up_ref), channel_id=1, source_target_pairs={{0,1},{1,2},{2,3},{3,4},{4,5},{5,6},{6,7},{8,9},{9,10},{10,11},{11... | collective-permute-start | bytes 798728 | tf_op jit(solution)/shard_map/ppermute | solution.py:324
  12.5 4.6 %collective-permute-start.95 = (f32[520,128]{1,0:T(8,128)}, f32[520,128]{1,0:T(8,128)S(1)}, u32[]{:S(2)}, u32[]{:S(2)}) collective-permute-start(f32[520,128]{1,0:T(8,128)} %get-tuple-element.472.down_ref), channel_id=1, source_target_pairs={{1,0},{2,1},{3,2},{4,3},{5,4},{6,5},{7,6},{9,8},{10,9},{11,10},{12... | collective-permute-start | bytes 798728 | tf_op jit(solution)/shard_map/ppermute | solution.py:325
  19.7 1.3 %align.2 = (f32[320,128]{1,0:T(8,128)S(1)}, f32[192,128]{1,0:T(8,128)S(1)}) custom-call(s32[2]{0:T(128)} %shift_ref.3, f32[2]{0:T(128)} %weight_ref.3, f32[520,128]{1,0:T(8,128)} %get-tuple-element.471.own_ref.up_ref, f32[584,128]{1,0:T(8,128)} %copy-done, f32[584,128]{1,0:T(8,128)} %copy-done.2), custom_call_target="tpu_custom_call" | custom-call | tf_op jit(solution)/shard_map/align/pallas_call | solution.py:131
  21.0 37.3 %conditional.32 = ((f32[320,128]{1,0:T(8,128)}, f32[192,128]{1,0:T(8,128)})) conditional(s32[]{:T(128)} %convert_element_type.96, (s32[]{:T(128)}, f32[320,128]{1,0:T(8,128)S(1)}, f32[192,128]{1,0:T(8,128)S(1)}) %tuple.205, (s32[]{:T(128)}, f32[320,128]{1,0:T(8,128)S(1)}, f32[192,128]{1,0:T(8,128)S(1)}) %tuple.205), branch_computations={%region_0.0_spmd, %region_17.0_spmd} | conditional | flops 8 | bytes 1441994 | solution.py:294
  21.6 36.7 %conditional.7 = ((f32[320,128]{1,0:T(8,128)}, f32[192,128]{1,0:T(8,128)})) conditional(s32[]{:T(128)} %convert_element_type.71, (s32[]{:T(128)}, f32[320,128]{1,0:T(8,128)S(1)}, f32[192,128]{1,0:T(8,128)S(1)}) %param.16, (s32[]{:T(128)}, f32[320,128]{1,0:T(8,128)S(1)}, f32[192,128]{1,0:T(8,128)S(1)}) %param.16), branch_computations={%region_1.0_spmd, %region_10.0_spmd} | conditional | flops 6 | bytes 1441980 | solution.py:294
  22.2 36.1 %conditional.6 = ((f32[320,128]{1,0:T(8,128)}, f32[192,128]{1,0:T(8,128)})) conditional(s32[]{:T(128)} %convert_element_type.70, (s32[]{:T(128)}, f32[320,128]{1,0:T(8,128)S(1)}, f32[192,128]{1,0:T(8,128)S(1)}) %param.15, (s32[]{:T(128)}, f32[320,128]{1,0:T(8,128)S(1)}, f32[192,128]{1,0:T(8,128)S(1)}) %param.15), branch_computations={%region_11.0_spmd, %region_14.0_spmd} | conditional | flops 2 | bytes 1441966 | solution.py:294
  22.8 35.5 %conditional.5 = (f32[320,128]{1,0:T(8,128)}, f32[192,128]{1,0:T(8,128)}) conditional(s32[]{:T(128)} %convert_element_type.69, (f32[320,128]{1,0:T(8,128)S(1)}, f32[192,128]{1,0:T(8,128)S(1)}) %tuple.149, (f32[320,128]{1,0:T(8,128)S(1)}, f32[192,128]{1,0:T(8,128)S(1)}) %tuple.149), branch_computations={%region_15.0_spmd, %region_16.0_spmd} | conditional | bytes 1441928 | solution.py:294
  22.8 2.7 %collective-permute-start.20 = (f32[192,128]{1,0:T(8,128)S(1)}, f32[192,128]{1,0:T(8,128)S(1)}, u32[]{:S(2)}, u32[]{:S(2)}) collective-permute-start(f32[192,128]{1,0:T(8,128)S(1)} %get-tuple-element.349), channel_id=1, source_target_pairs={{7,263},{15,271},{23,279},{31,287},{39,295},{47,303},{55,311},{63,... | collective-permute-start | bytes 294920 | tf_op jit(solution)/shard_map/cond/branch_0_fun/cond/branch_1_fun/cond/branch_1_fun/cond/branch_0_fun/ppermute | solution.py:285
  25.5 6.6 %collective-permute-start.19 = (f32[320,128]{1,0:T(8,128)S(1)}, f32[320,128]{1,0:T(8,128)}, u32[]{:S(2)}, u32[]{:S(2)}) collective-permute-start(f32[320,128]{1,0:T(8,128)S(1)} %get-tuple-element.348), channel_id=1, source_target_pairs={{7,407},{15,415},{23,423},{31,431},{39,439},{47,447},{55,455},{63,... | collective-permute-start | bytes 491528 | tf_op jit(solution)/shard_map/cond/branch_0_fun/cond/branch_1_fun/cond/branch_1_fun/cond/branch_0_fun/ppermute | solution.py:286
  32.2 7.7 %collective-permute-start.21 = (f32[192,128]{1,0:T(8,128)S(1)}, f32[192,128]{1,0:T(8,128)}, u32[]{:S(2)}, u32[]{:S(2)}) collective-permute-start(f32[192,128]{1,0:T(8,128)S(1)} %collective-permute-done.20), channel_id=1, source_target_pairs={{7,119},{15,127},{23,135},{31,143},{39,151},{47,159},{55,167},{63,... | collective-permute-start | bytes 294920 | tf_op jit(solution)/shard_map/cond/branch_0_fun/cond/branch_1_fun/cond/branch_1_fun/cond/branch_0_fun/ppermute | solution.py:287
  39.9 18.5 %collective-permute-done.19 = f32[320,128]{1,0:T(8,128)} collective-permute-done((f32[320,128]{1,0:T(8,128)S(1)}, f32[320,128]{1,0:T(8,128)}, u32[]{:S(2)}, u32[]{:S(2)}) %collective-permute-start.19) | collective-permute-done | bytes 163872 | tf_op jit(solution)/shard_map/cond/branch_0_fun/cond/branch_1_fun/cond/branch_1_fun/cond/branch_0_fun/ppermute | solution.py:286
  58.4 1.0 copy-done.3
  59.4 1.6 %substep.2 = (f32[512,128]{1,0:T(8,128)S(1)}, f32[512,128]{1,0:T(8,128)S(1)}, f32[576,128]{1,0:T(8,128)S(1)}, f32[576,128]{1,0:T(8,128)S(1)}) custom-call(f32[520,128]{1,0:T(8,128)S(1)} %copy-done.9, f32[520,128]{1,0:T(8,128)S(1)} %copy-done.12, f32[584,128]{1,0:T(8,128)S(1)} %copy-done.1, f32[584,128]{1,0:T(8,128)S(1)} %copy-done.3, ...), custom_call_target="tpu_custom_call" | custom-call | tf_op jit(solution)/shard_map/substep/pallas_call | solution.py:261
  61.0 2.9 %collective-permute-start.97 = (f32[576,128]{1,0:T(8,128)S(1)}, f32[576,128]{1,0:T(8,128)S(1)}, u32[]{:S(2)}, u32[]{:S(2)}) collective-permute-start(f32[576,128]{1,0:T(8,128)S(1)} %get-tuple-element.482), channel_id=1, source_target_pairs={{0,248},{1,249},{2,250},{3,251},{4,252},{5,253},{6,254},{7,255},{8... | collective-permute-start | bytes 884744 | tf_op jit(solution)/shard_map/ppermute | solution.py:323
  64.0 1.3 %collective-permute-start.98 = (f32[512,128]{1,0:T(8,128)S(1)}, f32[512,128]{1,0:T(8,128)S(1)}, u32[]{:S(2)}, u32[]{:S(2)}) collective-permute-start(f32[512,128]{1,0:T(8,128)S(1)} %get-tuple-element.479.own_ref.up_ref), channel_id=1, source_target_pairs={{0,1},{1,2},{2,3},{3,4},{4,5},{5,6},{6,7},{8,9},{9,10},{10,11},{11... | collective-permute-start | bytes 786440 | tf_op jit(solution)/shard_map/ppermute | solution.py:324
  65.3 4.6 %collective-permute-start.99 = (f32[512,128]{1,0:T(8,128)S(1)}, f32[512,128]{1,0:T(8,128)S(1)}, u32[]{:S(2)}, u32[]{:S(2)}) collective-permute-start(f32[512,128]{1,0:T(8,128)S(1)} %get-tuple-element.480.down_ref), channel_id=1, source_target_pairs={{1,0},{2,1},{3,2},{4,3},{5,4},{6,5},{7,6},{9,8},{10,9},{11,10},{12... | collective-permute-start | bytes 786440 | tf_op jit(solution)/shard_map/ppermute | solution.py:325
  71.8 1.2 %align.3 = (f32[320,128]{1,0:T(8,128)S(1)}, f32[192,128]{1,0:T(8,128)S(1)}) custom-call(s32[2]{0:T(128)} %shift_ref.3, f32[2]{0:T(128)} %weight_ref.3, f32[512,128]{1,0:T(8,128)} %copy-done.10, f32[576,128]{1,0:T(8,128)} %copy-done.5, f32[576,128]{1,0:T(8,128)} %copy-done.7), custom_call_target="tpu_custom_call" | custom-call | tf_op jit(solution)/shard_map/align/pallas_call | solution.py:131
  73.1 32.3 %conditional.33 = ((f32[320,128]{1,0:T(8,128)}, f32[192,128]{1,0:T(8,128)})) conditional(s32[]{:T(128)} %convert_element_type.97, (s32[]{:T(128)}, f32[320,128]{1,0:T(8,128)S(1)}, f32[192,128]{1,0:T(8,128)S(1)}) %tuple.206, (s32[]{:T(128)}, f32[320,128]{1,0:T(8,128)S(1)}, f32[192,128]{1,0:T(8,128)S(1)}) %tuple.206), branch_computations={%region_32.0_spmd, %region_49.0_spmd} | conditional | flops 8 | bytes 1441994 | solution.py:294
  73.7 31.7 %conditional.29 = ((f32[320,128]{1,0:T(8,128)}, f32[192,128]{1,0:T(8,128)})) conditional(s32[]{:T(128)} %convert_element_type.93, (s32[]{:T(128)}, f32[320,128]{1,0:T(8,128)S(1)}, f32[192,128]{1,0:T(8,128)S(1)}) %param.63, (s32[]{:T(128)}, f32[320,128]{1,0:T(8,128)S(1)}, f32[192,128]{1,0:T(8,128)S(1)}) %param.63), branch_computations={%region_50.0_spmd, %region_57.0_spmd} | conditional | flops 4 | bytes 1441980 | solution.py:294
  74.3 31.1 %conditional.25 = ((f32[320,128]{1,0:T(8,128)}, f32[192,128]{1,0:T(8,128)})) conditional(s32[]{:T(128)} %convert_element_type.89, (s32[]{:T(128)}, f32[320,128]{1,0:T(8,128)S(1)}, f32[192,128]{1,0:T(8,128)S(1)}) %param.55, (s32[]{:T(128)}, f32[320,128]{1,0:T(8,128)S(1)}, f32[192,128]{1,0:T(8,128)S(1)}) %param.55), branch_computations={%region_51.0_spmd, %region_54.0_spmd} | conditional | flops 2 | bytes 1441966 | solution.py:294
  74.9 30.5 %conditional.24 = (f32[320,128]{1,0:T(8,128)}, f32[192,128]{1,0:T(8,128)}) conditional(s32[]{:T(128)} %convert_element_type.88, (f32[320,128]{1,0:T(8,128)S(1)}, f32[192,128]{1,0:T(8,128)S(1)}) %tuple.191, (f32[320,128]{1,0:T(8,128)S(1)}, f32[192,128]{1,0:T(8,128)S(1)}) %tuple.191), branch_computations={%region_55.0_spmd, %region_56.0_spmd} | conditional | bytes 1441928 | solution.py:294
  74.9 1.9 %collective-permute-start.77 = (f32[192,128]{1,0:T(8,128)S(1)}, f32[192,128]{1,0:T(8,128)S(1)}, u32[]{:S(2)}, u32[]{:S(2)}) collective-permute-start(f32[192,128]{1,0:T(8,128)S(1)} %get-tuple-element.432), channel_id=1, source_target_pairs={{7,263},{15,271},{23,279},{31,287},{39,295},{47,303},{55,311},{63,... | collective-permute-start | bytes 294920 | tf_op jit(solution)/shard_map/cond/branch_1_fun/cond/branch_0_fun/cond/branch_1_fun/cond/branch_0_fun/ppermute | solution.py:285
  76.8 10.7 %collective-permute-start.76 = (f32[320,128]{1,0:T(8,128)S(1)}, f32[320,128]{1,0:T(8,128)}, u32[]{:S(2)}, u32[]{:S(2)}) collective-permute-start(f32[320,128]{1,0:T(8,128)S(1)} %get-tuple-element.431), channel_id=1, source_target_pairs={{7,343},{15,351},{23,359},{31,367},{39,375},{47,383},{55,391},{63,... | collective-permute-start | bytes 491528 | tf_op jit(solution)/shard_map/cond/branch_1_fun/cond/branch_0_fun/cond/branch_1_fun/cond/branch_0_fun/ppermute | solution.py:286
  87.5 1.9 %collective-permute-start.78 = (f32[192,128]{1,0:T(8,128)S(1)}, f32[192,128]{1,0:T(8,128)}, u32[]{:S(2)}, u32[]{:S(2)}) collective-permute-start(f32[192,128]{1,0:T(8,128)S(1)} %collective-permute-done.77), channel_id=1, source_target_pairs={{7,183},{15,191},{23,199},{31,207},{39,215},{47,223},{55,231},{63,... | collective-permute-start | bytes 294920 | tf_op jit(solution)/shard_map/cond/branch_1_fun/cond/branch_0_fun/cond/branch_1_fun/cond/branch_0_fun/ppermute | solution.py:287
  89.4 14.7 %collective-permute-done.76 = f32[320,128]{1,0:T(8,128)} collective-permute-done((f32[320,128]{1,0:T(8,128)S(1)}, f32[320,128]{1,0:T(8,128)}, u32[]{:S(2)}, u32[]{:S(2)}) %collective-permute-start.76) | collective-permute-done | bytes 163872 | tf_op jit(solution)/shard_map/cond/branch_1_fun/cond/branch_0_fun/cond/branch_1_fun/cond/branch_0_fun/ppermute | solution.py:286
  104.1 1.3 %collective-permute-done.78 = f32[192,128]{1,0:T(8,128)} collective-permute-done((f32[192,128]{1,0:T(8,128)S(1)}, f32[192,128]{1,0:T(8,128)}, u32[]{:S(2)}, u32[]{:S(2)}) %collective-permute-start.78) | collective-permute-done | bytes 98336 | tf_op jit(solution)/shard_map/cond/branch_1_fun/cond/branch_0_fun/cond/branch_1_fun/cond/branch_0_fun/ppermute | solution.py:287
  105.4 1.0 copy-done.6
  106.4 1.0 copy-done.8
  107.3 0.9 copy-done.11
  108.3 2.5 %substep.3 = f32[1024,128]{1,0:T(8,128)} custom-call(f32[512,128]{1,0:T(8,128)S(1)} %copy-done.11, f32[512,128]{1,0:T(8,128)S(1)} %get-tuple-element.480.down_ref, f32[576,128]{1,0:T(8,128)S(1)} %copy-done.6, f32[576,128]{1,0:T(8,128)S(1)} %copy-done.8, f32[512,128]{1,0:T(8,128)S(1)} %collective-permute-done.98.below_ref, ...), custom_call_target="tpu_custom_call" | custom-call | tf_op jit(solution)/shard_map/substep/pallas_call | solution.py:261
  (46 shorter events, 3.5 us)
Async XLA Ops:
  2.1 16.1 %collective-permute-start.92 = (f32[584,128]{1,0:T(8,128)}, f32[584,128]{1,0:T(8,128)S(1)}, u32[]{:S(2)}, u32[]{:S(2)}) collective-permute-start(f32[584,128]{1,0:T(8,128)} %get-tuple-element.473), channel_id=1, source_target_pairs={{0,8},{1,9},{2,10},{3,11},{4,12},{5,13},{6,14},{7,15},{8,16},{9,17... | collective-permute-start | bytes 897032 | tf_op jit(solution)/shard_map/ppermute | solution.py:322
  2.1 16.1 %collective-permute-start.93 = (f32[584,128]{1,0:T(8,128)}, f32[584,128]{1,0:T(8,128)S(1)}, u32[]{:S(2)}, u32[]{:S(2)}) collective-permute-start(f32[584,128]{1,0:T(8,128)} %get-tuple-element.474), channel_id=1, source_target_pairs={{0,248},{1,249},{2,250},{3,251},{4,252},{5,253},{6,254},{7,255},{8... | collective-permute-start | bytes 897032 | tf_op jit(solution)/shard_map/ppermute | solution.py:323
  11.1 6.0 %copy-start.17 = (s32[2]{0:T(128)S(1)}, s32[2]{0:T(128)}, u32[]{:S(2)}) copy-start(s32[2]{0:T(128)} %shift_ref.3) | copy-start | bytes 28
  11.1 47.3 %collective-permute-start.94 = (f32[520,128]{1,0:T(8,128)}, f32[520,128]{1,0:T(8,128)S(1)}, u32[]{:S(2)}, u32[]{:S(2)}) collective-permute-start(f32[520,128]{1,0:T(8,128)} %get-tuple-element.471.own_ref.up_ref), channel_id=1, source_target_pairs={{0,1},{1,2},{2,3},{3,4},{4,5},{5,6},{6,7},{8,9},{9,10},{10,11},{11... | collective-permute-start | bytes 798728 | tf_op jit(solution)/shard_map/ppermute | solution.py:324
  12.5 45.9 %collective-permute-start.95 = (f32[520,128]{1,0:T(8,128)}, f32[520,128]{1,0:T(8,128)S(1)}, u32[]{:S(2)}, u32[]{:S(2)}) collective-permute-start(f32[520,128]{1,0:T(8,128)} %get-tuple-element.472.down_ref), channel_id=1, source_target_pairs={{1,0},{2,1},{3,2},{4,3},{5,4},{6,5},{7,6},{9,8},{10,9},{11,10},{12... | collective-permute-start | bytes 798728 | tf_op jit(solution)/shard_map/ppermute | solution.py:325
  18.2 0.7 copy-start
  18.9 0.7 copy-start.2
  19.7 38.7 %copy-start.9 = (f32[520,128]{1,0:T(8,128)S(1)}, f32[520,128]{1,0:T(8,128)}, u32[]{:S(2)}) copy-start(f32[520,128]{1,0:T(8,128)} %get-tuple-element.471.own_ref.up_ref) | copy-start | bytes 798724
  19.7 38.7 %copy-start.12 = (f32[520,128]{1,0:T(8,128)S(1)}, f32[520,128]{1,0:T(8,128)}, u32[]{:S(2)}) copy-start(f32[520,128]{1,0:T(8,128)} %get-tuple-element.472.down_ref) | copy-start | bytes 798724
  19.7 38.7 %copy-start.14 = (f32[64,64]{1,0:T(8,128)S(1)}, f32[64,64]{1,0:T(8,128)}, u32[]{:S(2)}) copy-start(f32[64,64]{1,0:T(8,128)} %split_ref.3) | copy-start | bytes 49156
  19.7 38.7 %copy-start.15 = (f32[64,64]{1,0:T(8,128)S(1)}, f32[64,64]{1,0:T(8,128)}, u32[]{:S(2)}) copy-start(f32[64,64]{1,0:T(8,128)} %merge_ref.3) | copy-start | bytes 49156
  19.7 38.7 %copy-start.16 = (f32[1,2,8,128]{3,2,1,0:T(8,128)S(1)}, f32[1,2,8,128]{3,2,1,0:T(8,128)}, u32[]{:S(2)}) copy-start(f32[1,2,8,128]{3,2,1,0:T(8,128)} %param.73) | copy-start | bytes 24580
  21.0 37.4 %copy-start.1 = (f32[584,128]{1,0:T(8,128)S(1)}, f32[584,128]{1,0:T(8,128)}, u32[]{:S(2)}) copy-start(f32[584,128]{1,0:T(8,128)} %copy-done) | copy-start | bytes 897028
  21.0 37.4 %copy-start.13 = (f32[1,3,2,8,128]{4,3,2,1,0:T(8,128)S(1)}, f32[1,3,2,8,128]{4,3,2,1,0:T(8,128)}, u32[]{:S(2)}) copy-start(f32[1,3,2,8,128]{4,3,2,1,0:T(8,128)} %param.72) | copy-start | bytes 73732
  22.8 9.4 %collective-permute-start.20 = (f32[192,128]{1,0:T(8,128)S(1)}, f32[192,128]{1,0:T(8,128)S(1)}, u32[]{:S(2)}, u32[]{:S(2)}) collective-permute-start(f32[192,128]{1,0:T(8,128)S(1)} %get-tuple-element.349), channel_id=1, source_target_pairs={{7,263},{15,271},{23,279},{31,287},{39,295},{47,303},{55,311},{63,... | collective-permute-start | bytes 294920 | tf_op jit(solution)/shard_map/cond/branch_0_fun/cond/branch_1_fun/cond/branch_1_fun/cond/branch_0_fun/ppermute | solution.py:285
  25.5 32.8 %collective-permute-start.19 = (f32[320,128]{1,0:T(8,128)S(1)}, f32[320,128]{1,0:T(8,128)}, u32[]{:S(2)}, u32[]{:S(2)}) collective-permute-start(f32[320,128]{1,0:T(8,128)S(1)} %get-tuple-element.348), channel_id=1, source_target_pairs={{7,407},{15,415},{23,423},{31,431},{39,439},{47,447},{55,455},{63,... | collective-permute-start | bytes 491528 | tf_op jit(solution)/shard_map/cond/branch_0_fun/cond/branch_1_fun/cond/branch_1_fun/cond/branch_0_fun/ppermute | solution.py:286
  32.2 26.2 %collective-permute-start.21 = (f32[192,128]{1,0:T(8,128)S(1)}, f32[192,128]{1,0:T(8,128)}, u32[]{:S(2)}, u32[]{:S(2)}) collective-permute-start(f32[192,128]{1,0:T(8,128)S(1)} %collective-permute-done.20), channel_id=1, source_target_pairs={{7,119},{15,127},{23,135},{31,143},{39,151},{47,159},{55,167},{63,... | collective-permute-start | bytes 294920 | tf_op jit(solution)/shard_map/cond/branch_0_fun/cond/branch_1_fun/cond/branch_1_fun/cond/branch_0_fun/ppermute | solution.py:287
  58.4 1.0 copy-start.3
  61.0 9.4 %copy-start.10 = (f32[512,128]{1,0:T(8,128)}, f32[512,128]{1,0:T(8,128)S(1)}, u32[]{:S(2)}) copy-start(f32[512,128]{1,0:T(8,128)S(1)} %get-tuple-element.479.own_ref.up_ref) | copy-start | bytes 786436
  61.0 9.4 %collective-permute-start.96 = (f32[576,128]{1,0:T(8,128)S(1)}, f32[576,128]{1,0:T(8,128)S(1)}, u32[]{:S(2)}, u32[]{:S(2)}) collective-permute-start(f32[576,128]{1,0:T(8,128)S(1)} %get-tuple-element.481), channel_id=1, source_target_pairs={{0,8},{1,9},{2,10},{3,11},{4,12},{5,13},{6,14},{7,15},{8,16},{9,17... | collective-permute-start | bytes 884744 | tf_op jit(solution)/shard_map/ppermute | solution.py:322
  61.0 9.4 %collective-permute-start.97 = (f32[576,128]{1,0:T(8,128)S(1)}, f32[576,128]{1,0:T(8,128)S(1)}, u32[]{:S(2)}, u32[]{:S(2)}) collective-permute-start(f32[576,128]{1,0:T(8,128)S(1)} %get-tuple-element.482), channel_id=1, source_target_pairs={{0,248},{1,249},{2,250},{3,251},{4,252},{5,253},{6,254},{7,255},{8... | collective-permute-start | bytes 884744 | tf_op jit(solution)/shard_map/ppermute | solution.py:323
  64.0 41.4 %collective-permute-start.98 = (f32[512,128]{1,0:T(8,128)S(1)}, f32[512,128]{1,0:T(8,128)S(1)}, u32[]{:S(2)}, u32[]{:S(2)}) collective-permute-start(f32[512,128]{1,0:T(8,128)S(1)} %get-tuple-element.479.own_ref.up_ref), channel_id=1, source_target_pairs={{0,1},{1,2},{2,3},{3,4},{4,5},{5,6},{6,7},{8,9},{9,10},{10,11},{11... | collective-permute-start | bytes 786440 | tf_op jit(solution)/shard_map/ppermute | solution.py:324
  65.3 40.1 %collective-permute-start.99 = (f32[512,128]{1,0:T(8,128)S(1)}, f32[512,128]{1,0:T(8,128)S(1)}, u32[]{:S(2)}, u32[]{:S(2)}) collective-permute-start(f32[512,128]{1,0:T(8,128)S(1)} %get-tuple-element.480.down_ref), channel_id=1, source_target_pairs={{1,0},{2,1},{3,2},{4,3},{5,4},{6,5},{7,6},{9,8},{10,9},{11,10},{12... | collective-permute-start | bytes 786440 | tf_op jit(solution)/shard_map/ppermute | solution.py:325
  70.4 0.7 copy-start.5
  71.1 0.7 copy-start.7
  73.1 32.3 %copy-start.4 = (f32[584,128]{1,0:T(8,128)S(1)}, f32[584,128]{1,0:T(8,128)}, u32[]{:S(2)}) copy-start(f32[584,128]{1,0:T(8,128)} %copy-done.2) | copy-start | bytes 897028
  74.9 12.6 %collective-permute-start.77 = (f32[192,128]{1,0:T(8,128)S(1)}, f32[192,128]{1,0:T(8,128)S(1)}, u32[]{:S(2)}, u32[]{:S(2)}) collective-permute-start(f32[192,128]{1,0:T(8,128)S(1)} %get-tuple-element.432), channel_id=1, source_target_pairs={{7,263},{15,271},{23,279},{31,287},{39,295},{47,303},{55,311},{63,... | collective-permute-start | bytes 294920 | tf_op jit(solution)/shard_map/cond/branch_1_fun/cond/branch_0_fun/cond/branch_1_fun/cond/branch_0_fun/ppermute | solution.py:285
  76.8 27.3 %collective-permute-start.76 = (f32[320,128]{1,0:T(8,128)S(1)}, f32[320,128]{1,0:T(8,128)}, u32[]{:S(2)}, u32[]{:S(2)}) collective-permute-start(f32[320,128]{1,0:T(8,128)S(1)} %get-tuple-element.431), channel_id=1, source_target_pairs={{7,343},{15,351},{23,359},{31,367},{39,375},{47,383},{55,391},{63,... | collective-permute-start | bytes 491528 | tf_op jit(solution)/shard_map/cond/branch_1_fun/cond/branch_0_fun/cond/branch_1_fun/cond/branch_0_fun/ppermute | solution.py:286
  87.5 17.9 %collective-permute-start.78 = (f32[192,128]{1,0:T(8,128)S(1)}, f32[192,128]{1,0:T(8,128)}, u32[]{:S(2)}, u32[]{:S(2)}) collective-permute-start(f32[192,128]{1,0:T(8,128)S(1)} %collective-permute-done.77), channel_id=1, source_target_pairs={{7,183},{15,191},{23,199},{31,207},{39,215},{47,223},{55,231},{63,... | collective-permute-start | bytes 294920 | tf_op jit(solution)/shard_map/cond/branch_1_fun/cond/branch_0_fun/cond/branch_1_fun/cond/branch_0_fun/ppermute | solution.py:287
  105.4 1.0 copy-start.6
  106.4 1.0 copy-start.8
  107.3 0.9 copy-start.11
where the time goes:
time: 111 us
  starting transfers between devices  55.3 us (50%)
  waiting for transfers between devices  34.4 us (31%)
  Pallas kernels  8.72 us (8%)
  local copies, waits for them, and re-layouts  7.25 us (7%)
  loops' own time  3.66 us (3%)
  between operations  1.42 us (1%)
    ppermute x2, waiting for transfers between devices, turn(): direct = lax.ppermute(direct, AXES, turn_pairs(2 * chips, True))  33.1 us
    ppermute x2, starting transfers between devices, turn(): direct = lax.ppermute(direct, AXES, turn_pairs(2 * chips, True))  17.3 us
    ppermute x2, starting transfers between devices, body(): from_next = lax.ppermute(to_prev, AXES, sector_pairs(-1))  11.9 us
    ppermute x2, starting transfers between devices, turn(): cross = lax.ppermute(cross, AXES, turn_pairs(2 * chips, False))  9.61 us
    ppermute x2, starting transfers between devices, body(): above = lax.ppermute(down, AXES, block_pairs(-1))  9.12 us
    unnamed x36, local copies, waits for them, and re-layouts  6.68 us
    ppermute x2, starting transfers between devices, turn(): cross = lax.ppermute(cross, AXES, turn_pairs(0, True))  4.66 us
    pallas_call x2, Pallas kernels, run_substep(): pl.pallas_call(functools.partial(substep_kernel, final), out_shape=out_sh...  4.08 us
  transfers between devices with their start and end apart: 14, of which 3 were waited for; matrix products, arithmetic and copies ran while one was open for 1% of the time, Pallas kernels for 2%

commit v1 on v0

--- a/solution.py
+++ b/solution.py
@@ -8,6 +8,7 @@
 from jax.sharding import PartitionSpec as P
 
 TIME_STEP = 0.2
+GRANT = 8 * 1024 * 1024
 AXES = ("region", "sector", "block")
 SECTIONS = 64
 CELLS = 8
@@ -25,25 +26,22 @@
     return (region * lax.axis_size("sector") + sector) * lax.axis_size("block") + block
 
 
-def sector_pairs(step):
-    count = lax.axis_size("sector")
-    return [
-        (device_number(r, s, b), device_number(r, (s + step) % count, b))
-        for r in range(2)
-        for s in range(count)
-        for b in range(lax.axis_size("block"))
-    ]
-
-
-def block_pairs(step):
-    count = lax.axis_size("block")
-    return [
-        (device_number(r, s, b), device_number(r, s, b + step))
-        for r in range(2)
-        for s in range(lax.axis_size("sector"))
-        for b in range(count)
-        if 0 <= b + step < count
-    ]
+def swap_pairs(axis, first):
+    sectors, blocks = lax.axis_size("sector"), lax.axis_size("block")
+    pairs = []
+    for r in range(2):
+        for s in range(sectors):
+            for b in range(blocks):
+                if axis == "sector":
+                    step = 1 if s % 2 == first else -1
+                    to = device_number(r, (s + step) % sectors, b)
+                else:
+                    step = 1 if b % 2 == first else -1
+                    if not 0 <= b + step < blocks:
+                        continue
+                    to = device_number(r, s, b + step)
+                pairs.append((device_number(r, s, b), to))
+    return pairs
 
 
 def turn_pairs(sectors, across):
@@ -63,28 +61,51 @@
     return pl.ds(index * SECTIONS, SECTIONS)
 
 
-def pack_kernel(field_ref, speed_ref, up_ref, down_ref, next_ref, prev_ref):
-    for row, out_ref in ((0, down_ref), (1, up_ref)):
+def is_even(axis):
+    return lax.axis_index(axis) % 2 == 0
+
+
+def pack_kernel(field_ref, speed_ref, *out_refs):
+    for row in range(ROWS):
+        cells = [field_ref[pl.ds(row * CELLS + a, SECTIONS, stride=STRIDE), :] for a in range(CELLS)]
         for a in range(CELLS):
-            cells = field_ref[pl.ds(row * CELLS + a, SECTIONS, stride=STRIDE), :]
-            store_cells(row, a, cells, up_ref, down_ref, next_ref, prev_ref)
-        out_ref[pl.ds(ROW_BYTES_ROWS, CELLS), :] = speed_ref[pl.ds(STRIDE + row * CELLS, CELLS), :]
-    for edge_ref, a in ((prev_ref, 0), (next_ref, CELLS - 1)):
+            store_cells(row, a, cells[a], *out_refs)
+    _, _, first_block_ref, second_block_ref, first_sector_ref, second_sector_ref = out_refs
+    store_edge(lambda a: field_ref[pl.ds(a, SECTIONS, stride=STRIDE), :], first_sector_ref, second_sector_ref)
+    even_block, even_sector = is_even("block"), is_even("sector")
+    low, high = [speed_ref[pl.ds(STRIDE + row * CELLS, CELLS), :] for row in range(ROWS)]
+    first_block_ref[pl.ds(ROW_BYTES_ROWS, CELLS), :] = jnp.where(even_block, high, low)
+    second_block_ref[pl.ds(ROW_BYTES_ROWS, CELLS), :] = jnp.where(even_block, low, high)
+    for edge_ref, last_cell in ((first_sector_ref, even_sector), (second_sector_ref, jnp.logical_not(even_sector))):
         edge_ref[pl.ds(EDGE, 8), :] = jnp.zeros((8, AXIAL), jnp.float32)
         for row in range(ROWS):
-            edge_ref[pl.ds(EDGE + row, 1), :] = speed_ref[pl.ds(row * CELLS + a, 1), :]
-
-
-def store_cells(row, a, cells, up_ref, down_ref, next_ref, prev_ref):
+            a, z = [speed_ref[pl.ds(row * CELLS + place, 1), :] for place in (0, CELLS - 1)]
+            edge_ref[pl.ds(EDGE + row, 1), :] = jnp.where(last_cell, z, a)
+
+
+def store_cells(row, a, cells, low_ref, high_ref, first_block_ref, second_block_ref, first_sector_ref, second_sector_ref):
+    (low_ref, high_ref)[row][line(a), :] = cells
+    up_is_first = is_even("block")
+    goes_first = up_is_first if row else jnp.logical_not(up_is_first)
+
+    @pl.when(goes_first)
+    def _():
+        first_block_ref[line(a), :] = cells
+
+    @pl.when(jnp.logical_not(goes_first))
+    def _():
+        second_block_ref[line(a), :] = cells
+
     if row == ROWS - 1:
-        for out_ref in (up_ref, next_ref, prev_ref):
-            out_ref[line(a), :] = cells
-    else:
-        down_ref[line(a), :] = cells
-        if a == 0:
-            prev_ref[line(CELLS), :] = cells
-        if a == CELLS - 1:
-            next_ref[line(CELLS), :] = cells
+        first_sector_ref[line(a), :] = cells
+        second_sector_ref[line(a), :] = cells
+
+
+def store_edge(cells, first_sector_ref, second_sector_ref):
+    even = is_even("sector")
+    a, z = cells(0), cells(CELLS - 1)
+    first_sector_ref[line(CELLS), :] = jnp.where(even, z, a)
+    second_sector_ref[line(CELLS), :] = jnp.where(even, a, z)
 
 
 def lines(count):
@@ -96,25 +117,29 @@
 
 
 def pack(field, speeds):
+    row = lines(ROW_BYTES_ROWS)
     rim = lines(ROW_BYTES_ROWS + CELLS)
     edge = lines(EDGE + 8)
     return pl.pallas_call(
         pack_kernel,
-        out_shape=(rim, rim, edge, edge),
+        out_shape=(row, row, rim, rim, edge, edge),
         in_specs=vmem(2),
-        out_specs=tuple(vmem(4)),
+        out_specs=tuple(vmem(6)),
+        compiler_params=pltpu.CompilerParams(vmem_limit_bytes=GRANT),
         name="pack",
     )(field, speeds)
 
 
-def align_kernel(substep, shift_ref, weight_ref, own_ref, prev_ref, next_ref, direct_ref, cross_ref, row_ref):
+def align_kernel(substep, shift_ref, weight_ref, own_ref, first_ref, second_ref, direct_ref, cross_ref, row_ref):
     @pl.when(lax.axis_index("block") == lax.axis_size("block") - 1)
     def _():
         on_stator = lax.axis_index("region") == 1
         residual = (shift_ref[substep] + CELLS) % STRIDE - CELLS
         weight = weight_ref[substep]
-        for place, part_ref in enumerate((prev_ref, own_ref, next_ref)):
-            row_ref[pl.ds(place * ROW_BYTES_ROWS, ROW_BYTES_ROWS), :] = part_ref[pl.ds(0, ROW_BYTES_ROWS), :]
+        first_place = jnp.where(is_even("sector"), 2, 0)
+        for place, part_ref in ((first_place, first_ref), (1, own_ref), (2 - first_place, second_ref)):
+            start = pl.multiple_of(place * ROW_BYTES_ROWS, ROW_BYTES_ROWS)
+            row_ref[pl.ds(start, ROW_BYTES_ROWS), :] = part_ref[pl.ds(0, ROW_BYTES_ROWS), :]
         first = CELLS + jnp.where(on_stator, residual, -residual - 1)
         later_weight = jnp.where(on_stator, 1.0 - weight, weight)
 
@@ -127,15 +152,16 @@
             cross_ref[pl.ds(a * CROSS, CROSS), :] = ghost[OWN:]
 
 
-def align(substep, shifts, weights, own, from_prev, from_next):
+def align(substep, shifts, weights, own, first, second):
     return pl.pallas_call(
         functools.partial(align_kernel, substep),
         out_shape=(lines(CELLS * OWN), lines(CELLS * CROSS)),
         in_specs=[pl.BlockSpec(memory_space=pltpu.SMEM)] * 2 + vmem(3),
         out_specs=tuple(vmem(2)),
         scratch_shapes=[pltpu.VMEM((3 * ROW_BYTES_ROWS, AXIAL), jnp.float32)],
+        compiler_params=pltpu.CompilerParams(vmem_limit_bytes=GRANT),
         name="align",
-    )(shifts, weights, own, from_prev, from_next)
+    )(shifts, weights, own, first, second)
 
 
 def split_halves(value):
@@ -146,18 +172,18 @@
 
 def substep_kernel(
     final,
-    up_ref,
-    down_ref,
-    prev_ref,
-    next_ref,
-    below_ref,
-    above_ref,
+    low_ref,
+    high_ref,
+    first_sector_ref,
+    second_sector_ref,
+    first_block_ref,
+    second_block_ref,
     direct_ref,
     cross_ref,
-    prev_rim_ref,
-    next_rim_ref,
-    below_rim_ref,
-    above_rim_ref,
+    first_sector_rim_ref,
+    second_sector_rim_ref,
+    first_block_rim_ref,
+    second_block_rim_ref,
     speed_ref,
     strain_ref,
     split_ref,
@@ -171,8 +197,17 @@
     block = lax.axis_index("block")
     first_block = block == 0
     last_block = block == lax.axis_size("block") - 1
-    below_speed = below_rim_ref[pl.ds(ROW_BYTES_ROWS, CELLS), :]
-    above_speed = above_rim_ref[pl.ds(ROW_BYTES_ROWS, CELLS), :]
+    even_block, even_sector = is_even("block"), is_even("sector")
+
+    def by_block(lines_of, first_ref=first_block_ref, second_ref=second_block_ref):
+        one, two = first_ref[lines_of, :], second_ref[lines_of, :]
+        return jnp.where(even_block, one, two), jnp.where(even_block, two, one)
+
+    def by_sector(lines_of, first_ref=first_sector_ref, second_ref=second_sector_ref):
+        one, two = first_ref[lines_of, :], second_ref[lines_of, :]
+        return jnp.where(even_sector, one, two), jnp.where(even_sector, two, one)
+
+    above_speed, below_speed = by_block(pl.ds(ROW_BYTES_ROWS, CELLS), first_block_rim_ref, second_block_rim_ref)
 
     @pl.when(last_block)
     def _():
@@ -182,12 +217,14 @@
 
     @pl.when(jnp.logical_not(last_block))
     def _():
-        top_ref[...] = above_ref[pl.ds(0, ROW_BYTES_ROWS), :]
+        for a in range(CELLS):
+            top_ref[line(a), :] = by_block(line(a))[0]
 
     for row in range(ROWS):
         azim = speed_ref[pl.ds(row * CELLS, CELLS), :]
-        azim_next = jnp.concatenate([azim[1:], next_rim_ref[pl.ds(EDGE + row, 1), :]], axis=0)
-        azim_prev = jnp.concatenate([prev_rim_ref[pl.ds(EDGE + row, 1), :], azim[:-1]], axis=0)
+        after, before = by_sector(pl.ds(EDGE + row, 1), first_sector_rim_ref, second_sector_rim_ref)
+        azim_next = jnp.concatenate([azim[1:], after], axis=0)
+        azim_prev = jnp.concatenate([before, azim[:-1]], axis=0)
         azim_high = 0.5 * (azim + azim_next)
         azim_low = 0.5 * (azim_prev + azim)
         radial = speed_ref[pl.ds(STRIDE + row * CELLS, CELLS), :]
@@ -220,7 +257,7 @@
     left = jnp.concatenate([both_high, both_high, both_low], axis=1)
 
     for row in range(ROWS):
-        own_ref = (down_ref, up_ref)[row]
+        own_ref = (low_ref, high_ref)[row]
         for pair in range(CELLS // 2):
             cells_of = [own_ref[line(2 * pair + i), :] for i in range(2)]
             wide = jnp.concatenate(cells_of, axis=1)
@@ -234,11 +271,17 @@
                 joined = products[SECTIONS:, i * AXIAL : (i + 1) * AXIAL]
                 coef = lambda n: coef_ref[n, pl.ds(row * CELLS + a, 1), :]
                 if row == 0:
-                    outer, inner = up_ref[line(a), :], below_ref[line(a), :]
+                    outer, inner = high_ref[line(a), :], by_block(line(a))[1]
                 else:
-                    outer, inner = top_ref[line(a), :], down_ref[line(a), :]
-                later = next_ref[line(0 if row else CELLS), :] if a == CELLS - 1 else own_ref[line(a + 1), :]
-                earlier = prev_ref[line(CELLS - 1 if row else CELLS), :] if a == 0 else own_ref[line(a - 1), :]
+                    outer, inner = top_ref[line(a), :], low_ref[line(a), :]
+                if a == CELLS - 1:
+                    later = by_sector(line(0 if row else CELLS))[0]
+                else:
+                    later = own_ref[line(a + 1), :]
+                if a == 0:
+                    earlier = by_sector(line(CELLS - 1 if row else CELLS))[1]
+                else:
+                    earlier = own_ref[line(a - 1), :]
                 value = cells * (coef(6) + joined)
                 value = value + coef(7) * broken
                 value = value + (coef(0) * outer + coef(1) * inner)
@@ -250,14 +293,16 @@
                     out_ref[pl.ds(row * CELLS + a, SECTIONS, stride=STRIDE), :] = value
                 else:
                     store_cells(row, a, value, *new_refs)
+        if row == 0 and not final:
+            store_edge(lambda a: new_refs[0][line(a), :], *new_refs[4:])
 
 
 def run_substep(final, *arrays):
     if final:
         out_shape, out_specs = lines(SECTIONS * STRIDE), vmem(1)[0]
     else:
-        out_shape = (lines(ROW_BYTES_ROWS), lines(ROW_BYTES_ROWS), lines(EDGE), lines(EDGE))
-        out_specs = tuple(vmem(4))
+        out_shape = (lines(ROW_BYTES_ROWS),) * 4 + (lines(EDGE),) * 2
+        out_specs = tuple(vmem(6))
     return pl.pallas_call(
         functools.partial(substep_kernel, final),
         out_shape=out_shape,
@@ -267,7 +312,7 @@
             pltpu.VMEM((8, STRIDE, AXIAL), jnp.float32),
             pltpu.VMEM((ROW_BYTES_ROWS, AXIAL), jnp.float32),
         ],
-        compiler_params=pltpu.CompilerParams(vmem_limit_bytes=32 * 1024 * 1024),
+        compiler_params=pltpu.CompilerParams(vmem_limit_bytes=GRANT),
         name="substep",
     )(*arrays)
 
@@ -318,19 +363,17 @@
     arrays = pack(field, speeds)
     rims = None
     for substep in range(2):
-        up, down, to_next, to_prev = arrays
-        from_prev = lax.ppermute(to_next, AXES, sector_pairs(1))
-        from_next = lax.ppermute(to_prev, AXES, sector_pairs(-1))
-        below = lax.ppermute(up, AXES, block_pairs(1))
-        above = lax.ppermute(down, AXES, block_pairs(-1))
-        direct, cross = align(substep, shifts, weights, up, from_prev, from_next)
+        low, high, *sends = arrays
+        swaps = [("block", 0), ("block", 1), ("sector", 0), ("sector", 1)]
+        blocks_sectors = [lax.ppermute(sent, AXES, swap_pairs(*swap)) for sent, swap in zip(sends, swaps)]
+        halos = blocks_sectors[2:] + blocks_sectors[:2]
+        direct, cross = align(substep, shifts, weights, high, *halos[:2])
         direct, cross = turned(shifts[substep], direct, cross)
-        halos = (from_prev, from_next, below, above)
         rims = rims or halos
         arrays = run_substep(
             substep == 1,
-            up,
-            down,
+            low,
+            high,
             *halos,
             direct,
             cross,

time: 111 us -> 86.2 us (0.78)
  the two profiles are of different devices: /device:TPU:30 before, /device:TPU:94 now
where the time goes in v1:
time: 86.2 us; the launch traced here: 85.5 us
  starting transfers between devices  45.2 us (52%)
  waiting for transfers between devices  23.9 us (28%)
  Pallas kernels  8.14 us (9%)
  loops' own time  3.84 us (4%)
  local copies, waits for them, and re-layouts  3.06 us (4%)
  between operations  1.42 us (2%)
    ppermute x2, waiting for transfers between devices, turn(): direct = lax.ppermute(direct, AXES, turn_pairs(2 * chips, True))  15.8 us
    ppermute x8, starting transfers between devices, body(): lax.ppermute(sent, AXES, swap_pairs(*swap))  13.8 us
    ppermute x2, starting transfers between devices, turn(): direct = lax.ppermute(direct, AXES, turn_pairs(2 * chips, True))  12.1 us
    ppermute x2, starting transfers between devices, turn(): cross = lax.ppermute(cross, AXES, turn_pairs(2 * chips, False))  11.2 us
    ppermute x2, starting transfers between devices, turn(): cross = lax.ppermute(cross, AXES, turn_pairs(0, True))  8.03 us
    pallas_call x2, Pallas kernels, run_substep(): pl.pallas_call(functools.partial(substep_kernel, final), out_shape=out_sh...  6.52 us
    ppermute x8, waiting for transfers between devices, body(): lax.ppermute(sent, AXES, swap_pairs(*swap))  4.25 us
    ppermute x2, waiting for transfers between devices, turn(): cross = lax.ppermute(cross, AXES, turn_pairs(2 * chips, False))  3.85 us
  transfers between devices with their start and end apart: 14, of which 5 were waited for; matrix products, arithmetic and copies ran while one was open for 1% of the time, Pallas kernels for 2%

profile of v1, /device:TPU:94, one launch (start us, length us, event | category | flops | bytes accessed | tf_op | source)
XLA Modules:
  0.0 85.5 jit_solution(11345756760637208515)
XLA Ops:
  0.0 1.0 %copy-done = f32[1,64,2,8,128]{4,3,2,1,0:T(8,128)S(1)} copy-done((f32[1,64,2,8,128]{4,3,2,1,0:T(8,128)S(1)}, f32[1,64,2,8,128]{4,3,2,1,0:T(8,128)}, u32[]{:S(2)}) %copy-start) | copy-done | bytes 524312
  1.0 0.7 copy-done.1
  2.1 1.9 %collective-permute-start.92 = (f32[584,128]{1,0:T(8,128)S(1)}, f32[584,128]{1,0:T(8,128)S(1)}, u32[]{:S(2)}, u32[]{:S(2)}) collective-permute-start(f32[584,128]{1,0:T(8,128)S(1)} %get-tuple-element.477), channel_id=1, source_target_pairs={{0,8},{1,9},{2,10},{3,11},{4,12},{5,13},{6,14},{7,15},{8,0},{9,1},... | collective-permute-start | bytes 897032 | tf_op jit(solution)/shard_map/ppermute | solution.py:368
  4.0 2.1 %collective-permute-start.93 = (f32[584,128]{1,0:T(8,128)S(1)}, f32[584,128]{1,0:T(8,128)S(1)}, u32[]{:S(2)}, u32[]{:S(2)}) collective-permute-start(f32[584,128]{1,0:T(8,128)S(1)} %get-tuple-element.478), channel_id=1, source_target_pairs={{0,248},{1,249},{2,250},{3,251},{4,252},{5,253},{6,254},{7,255},{8... | collective-permute-start | bytes 897032 | tf_op jit(solution)/shard_map/ppermute | solution.py:368
  6.2 2.7 %collective-permute-start.94 = (f32[520,128]{1,0:T(8,128)S(1)}, f32[520,128]{1,0:T(8,128)S(1)}, u32[]{:S(2)}, u32[]{:S(2)}) collective-permute-start(f32[520,128]{1,0:T(8,128)S(1)} %get-tuple-element.479), channel_id=1, source_target_pairs={{0,1},{1,0},{2,3},{3,2},{4,5},{5,4},{6,7},{7,6},{8,9},{9,8},{10,11... | collective-permute-start | bytes 798728 | tf_op jit(solution)/shard_map/ppermute | solution.py:368
  8.8 0.7 collective-permute-start.95
  10.8 1.3 %collective-permute-done.93.second_ref.second_sector_ref.second_sector_rim_ref = f32[584,128]{1,0:T(8,128)S(1)} collective-permute-done((f32[584,128]{1,0:T(8,128)S(1)}, f32[584,128]{1,0:T(8,128)S(1)}, u32[]{:S(2)}, u32[]{:S(2)}) %collective-permute-start.93) | collective-permute-done | bytes 299040 | tf_op jit(solution)/shard_map/ppermute | solution.py:368
  12.8 28.4 %conditional.32 = ((f32[320,128]{1,0:T(8,128)}, f32[192,128]{1,0:T(8,128)})) conditional(s32[]{:T(128)} %convert_element_type.96, (s32[]{:T(128)}, f32[320,128]{1,0:T(8,128)S(1)}, f32[192,128]{1,0:T(8,128)S(1)}) %tuple.205, (s32[]{:T(128)}, f32[320,128]{1,0:T(8,128)S(1)}, f32[192,128]{1,0:T(8,128)S(1)}) %tuple.205), branch_computations={%region_0.0_spmd, %region_17.0_spmd} | conditional | flops 8 | bytes 1441994 | solution.py:339
  13.5 27.8 %conditional.7 = ((f32[320,128]{1,0:T(8,128)}, f32[192,128]{1,0:T(8,128)})) conditional(s32[]{:T(128)} %convert_element_type.71, (s32[]{:T(128)}, f32[320,128]{1,0:T(8,128)S(1)}, f32[192,128]{1,0:T(8,128)S(1)}) %param.16, (s32[]{:T(128)}, f32[320,128]{1,0:T(8,128)S(1)}, f32[192,128]{1,0:T(8,128)S(1)}) %param.16), branch_computations={%region_1.0_spmd, %region_10.0_spmd} | conditional | flops 6 | bytes 1441980 | solution.py:339
  14.1 27.1 %conditional.3 = ((f32[320,128]{1,0:T(8,128)}, f32[192,128]{1,0:T(8,128)})) conditional(s32[]{:T(128)} %convert_element_type.67, (s32[]{:T(128)}, f32[320,128]{1,0:T(8,128)S(1)}, f32[192,128]{1,0:T(8,128)S(1)}) %param.8, (s32[]{:T(128)}, f32[320,128]{1,0:T(8,128)S(1)}, f32[192,128]{1,0:T(8,128)S(1)}) %param.8), branch_computations={%region_2.0_spmd, %region_7.0_spmd} | conditional | flops 4 | bytes 1441966 | solution.py:339
  14.8 26.4 %conditional.2 = (f32[320,128]{1,0:T(8,128)}, f32[192,128]{1,0:T(8,128)}) conditional(s32[]{:T(128)} %convert_element_type.66, (f32[320,128]{1,0:T(8,128)S(1)}, f32[192,128]{1,0:T(8,128)S(1)}) %tuple.141, (f32[320,128]{1,0:T(8,128)S(1)}, f32[192,128]{1,0:T(8,128)S(1)}) %tuple.141), branch_computations={%region_8.0_spmd, %region_9.0_spmd} | conditional | bytes 1441928 | solution.py:339
  14.8 2.7 %collective-permute-start.8 = (f32[192,128]{1,0:T(8,128)S(1)}, f32[192,128]{1,0:T(8,128)S(1)}, u32[]{:S(2)}, u32[]{:S(2)}) collective-permute-start(f32[192,128]{1,0:T(8,128)S(1)} %get-tuple-element.334), channel_id=1, source_target_pairs={{7,263},{15,271},{23,279},{31,287},{39,295},{47,303},{55,311},{63,... | collective-permute-start | bytes 294920 | tf_op jit(solution)/shard_map/cond/branch_0_fun/cond/branch_0_fun/cond/branch_1_fun/cond/branch_0_fun/ppermute | solution.py:330
  17.6 8.4 %collective-permute-start.7 = (f32[320,128]{1,0:T(8,128)S(1)}, f32[320,128]{1,0:T(8,128)}, u32[]{:S(2)}, u32[]{:S(2)}) collective-permute-start(f32[320,128]{1,0:T(8,128)S(1)} %get-tuple-element.333), channel_id=1, source_target_pairs={{7,471},{15,479},{23,487},{31,495},{39,503},{47,511},{55,263},{63,... | collective-permute-start | bytes 491528 | tf_op jit(solution)/shard_map/cond/branch_0_fun/cond/branch_0_fun/cond/branch_1_fun/cond/branch_0_fun/ppermute | solution.py:331
  26.0 6.7 %collective-permute-start.9 = (f32[192,128]{1,0:T(8,128)S(1)}, f32[192,128]{1,0:T(8,128)}, u32[]{:S(2)}, u32[]{:S(2)}) collective-permute-start(f32[192,128]{1,0:T(8,128)S(1)} %collective-permute-done.8), channel_id=1, source_target_pairs={{7,55},{15,63},{23,71},{31,79},{39,87},{47,95},{55,103},{63,111},{... | collective-permute-start | bytes 294920 | tf_op jit(solution)/shard_map/cond/branch_0_fun/cond/branch_0_fun/cond/branch_1_fun/cond/branch_0_fun/ppermute | solution.py:332
  32.6 4.8 %collective-permute-done.7 = f32[320,128]{1,0:T(8,128)} collective-permute-done((f32[320,128]{1,0:T(8,128)S(1)}, f32[320,128]{1,0:T(8,128)}, u32[]{:S(2)}, u32[]{:S(2)}) %collective-permute-start.7) | collective-permute-done | bytes 163872 | tf_op jit(solution)/shard_map/cond/branch_0_fun/cond/branch_0_fun/cond/branch_1_fun/cond/branch_0_fun/ppermute | solution.py:331
  37.4 3.8 %collective-permute-done.9 = f32[192,128]{1,0:T(8,128)} collective-permute-done((f32[192,128]{1,0:T(8,128)S(1)}, f32[192,128]{1,0:T(8,128)}, u32[]{:S(2)}, u32[]{:S(2)}) %collective-permute-start.9) | collective-permute-done | bytes 98336 | tf_op jit(solution)/shard_map/cond/branch_0_fun/cond/branch_0_fun/cond/branch_1_fun/cond/branch_0_fun/ppermute | solution.py:332
  41.3 0.7 copy-done.5
  42.0 4.0 %substep.2 = (f32[512,128]{1,0:T(8,128)S(1)}, f32[512,128]{1,0:T(8,128)S(1)}, f32[512,128]{1,0:T(8,128)}, f32[512,128]{1,0:T(8,128)}, f32[576,128]{1,0:T(8,128)S(1)}, /*index=5*/f32[576,128]{1,0:T(8,128)S(1)}) custom-call(f32[512,128]{1,0:T(8,128)S(1)} %get-tuple-element.475.low_ref, f32[512,128]{1,0:T(8,128)S(1)} %get-tuple-element.476.own_ref.high_ref, ...), custom_call_target="tpu_custom_call" | custom-call | tf_op jit(solution)/shard_map/substep/pallas_call | solution.py:306
  46.0 1.9 %collective-permute-start.96 = (f32[576,128]{1,0:T(8,128)S(1)}, f32[576,128]{1,0:T(8,128)S(1)}, u32[]{:S(2)}, u32[]{:S(2)}) collective-permute-start(f32[576,128]{1,0:T(8,128)S(1)} %get-tuple-element.487), channel_id=1, source_target_pairs={{0,8},{1,9},{2,10},{3,11},{4,12},{5,13},{6,14},{7,15},{8,0},{9,1},... | collective-permute-start | bytes 884744 | tf_op jit(solution)/shard_map/ppermute | solution.py:368
  47.9 1.9 %collective-permute-start.97 = (f32[576,128]{1,0:T(8,128)S(1)}, f32[576,128]{1,0:T(8,128)S(1)}, u32[]{:S(2)}, u32[]{:S(2)}) collective-permute-start(f32[576,128]{1,0:T(8,128)S(1)} %get-tuple-element.488), channel_id=1, source_target_pairs={{0,248},{1,249},{2,250},{3,251},{4,252},{5,253},{6,254},{7,255},{8... | collective-permute-start | bytes 884744 | tf_op jit(solution)/shard_map/ppermute | solution.py:368
  49.8 1.9 %collective-permute-start.98 = (f32[512,128]{1,0:T(8,128)}, f32[512,128]{1,0:T(8,128)S(1)}, u32[]{:S(2)}, u32[]{:S(2)}) collective-permute-start(f32[512,128]{1,0:T(8,128)} %get-tuple-element.489), channel_id=1, source_target_pairs={{0,1},{1,0},{2,3},{3,2},{4,5},{5,4},{6,7},{7,6},{8,9},{9,8},{10,11... | collective-permute-start | bytes 786440 | tf_op jit(solution)/shard_map/ppermute | solution.py:368
  51.7 0.7 collective-permute-start.99
  53.0 2.9 %collective-permute-done.97.second_ref.second_sector_ref = f32[576,128]{1,0:T(8,128)S(1)} collective-permute-done((f32[576,128]{1,0:T(8,128)S(1)}, f32[576,128]{1,0:T(8,128)S(1)}, u32[]{:S(2)}, u32[]{:S(2)}) %collective-permute-start.97) | collective-permute-done | bytes 294944 | tf_op jit(solution)/shard_map/ppermute | solution.py:368
  56.6 26.4 %conditional.33 = ((f32[320,128]{1,0:T(8,128)}, f32[192,128]{1,0:T(8,128)})) conditional(s32[]{:T(128)} %convert_element_type.97, (s32[]{:T(128)}, f32[320,128]{1,0:T(8,128)S(1)}, f32[192,128]{1,0:T(8,128)S(1)}) %tuple.206, (s32[]{:T(128)}, f32[320,128]{1,0:T(8,128)S(1)}, f32[192,128]{1,0:T(8,128)S(1)}) %tuple.206), branch_computations={%region_32.0_spmd, %region_49.0_spmd} | conditional | flops 8 | bytes 1441994 | solution.py:339
  57.2 25.8 %conditional.29 = ((f32[320,128]{1,0:T(8,128)}, f32[192,128]{1,0:T(8,128)})) conditional(s32[]{:T(128)} %convert_element_type.93, (s32[]{:T(128)}, f32[320,128]{1,0:T(8,128)S(1)}, f32[192,128]{1,0:T(8,128)S(1)}) %param.63, (s32[]{:T(128)}, f32[320,128]{1,0:T(8,128)S(1)}, f32[192,128]{1,0:T(8,128)S(1)}) %param.63), branch_computations={%region_50.0_spmd, %region_57.0_spmd} | conditional | flops 4 | bytes 1441980 | solution.py:339
  57.8 25.2 %conditional.28 = ((f32[320,128]{1,0:T(8,128)}, f32[192,128]{1,0:T(8,128)})) conditional(s32[]{:T(128)} %convert_element_type.92, (s32[]{:T(128)}, f32[320,128]{1,0:T(8,128)S(1)}, f32[192,128]{1,0:T(8,128)S(1)}) %param.62, (s32[]{:T(128)}, f32[320,128]{1,0:T(8,128)S(1)}, f32[192,128]{1,0:T(8,128)S(1)}) %param.62), branch_computations={%region_58.0_spmd, %region_61.0_spmd} | conditional | flops 2 | bytes 1441966 | solution.py:339
  58.3 24.6 %conditional.26 = (f32[320,128]{1,0:T(8,128)}, f32[192,128]{1,0:T(8,128)}) conditional(s32[]{:T(128)} %convert_element_type.90, (f32[320,128]{1,0:T(8,128)S(1)}, f32[192,128]{1,0:T(8,128)S(1)}) %tuple.195, (f32[320,128]{1,0:T(8,128)S(1)}, f32[192,128]{1,0:T(8,128)S(1)}) %tuple.195), branch_computations={%region_59.0_spmd, %region_60.0_spmd} | conditional | bytes 1441928 | solution.py:339
  58.3 5.3 %collective-permute-start.83 = (f32[192,128]{1,0:T(8,128)S(1)}, f32[192,128]{1,0:T(8,128)S(1)}, u32[]{:S(2)}, u32[]{:S(2)}) collective-permute-start(f32[192,128]{1,0:T(8,128)S(1)} %get-tuple-element.440), channel_id=1, source_target_pairs={{7,263},{15,271},{23,279},{31,287},{39,295},{47,303},{55,311},{63,... | collective-permute-start | bytes 294920 | tf_op jit(solution)/shard_map/cond/branch_1_fun/cond/branch_1_fun/cond/branch_0_fun/cond/branch_0_fun/ppermute | solution.py:330
  63.6 3.8 %collective-permute-start.82 = (f32[320,128]{1,0:T(8,128)S(1)}, f32[320,128]{1,0:T(8,128)}, u32[]{:S(2)}, u32[]{:S(2)}) collective-permute-start(f32[320,128]{1,0:T(8,128)S(1)} %get-tuple-element.439), channel_id=1, source_target_pairs={{7,311},{15,319},{23,327},{31,335},{39,343},{47,351},{55,359},{63,... | collective-permute-start | bytes 491528 | tf_op jit(solution)/shard_map/cond/branch_1_fun/cond/branch_1_fun/cond/branch_0_fun/cond/branch_0_fun/ppermute | solution.py:331
  67.4 4.5 %collective-permute-start.84 = (f32[192,128]{1,0:T(8,128)S(1)}, f32[192,128]{1,0:T(8,128)}, u32[]{:S(2)}, u32[]{:S(2)}) collective-permute-start(f32[192,128]{1,0:T(8,128)S(1)} %collective-permute-done.83), channel_id=1, source_target_pairs={{7,215},{15,223},{23,231},{31,239},{39,247},{47,255},{55,7},{63,15... | collective-permute-start | bytes 294920 | tf_op jit(solution)/shard_map/cond/branch_1_fun/cond/branch_1_fun/cond/branch_0_fun/cond/branch_0_fun/ppermute | solution.py:332
  72.0 11.0 %collective-permute-done.82 = f32[320,128]{1,0:T(8,128)} collective-permute-done((f32[320,128]{1,0:T(8,128)S(1)}, f32[320,128]{1,0:T(8,128)}, u32[]{:S(2)}, u32[]{:S(2)}) %collective-permute-start.82) | collective-permute-done | bytes 163872 | tf_op jit(solution)/shard_map/cond/branch_1_fun/cond/branch_1_fun/cond/branch_0_fun/cond/branch_0_fun/ppermute | solution.py:331
  83.0 2.5 %substep.3 = f32[1024,128]{1,0:T(8,128)} custom-call(f32[512,128]{1,0:T(8,128)S(1)} %get-tuple-element.485.low_ref, f32[512,128]{1,0:T(8,128)S(1)} %get-tuple-element.486.own_ref.high_ref, f32[576,128]{1,0:T(8,128)S(1)} %collective-permute-done.96.first_ref.first_sector_ref, f32[576,128]{1,0:T(8,128)S(1)} %collective-permute-done.97.second_ref.second_sector_ref, ...), custom_call_target="tpu_custom_call" | custom-call | tf_op jit(solution)/shard_map/substep/pallas_call | solution.py:306
  (26 shorter events, 2.3 us)
Async XLA Ops:
  0.0 1.0 %copy-start = (f32[1,64,2,8,128]{4,3,2,1,0:T(8,128)S(1)}, f32[1,64,2,8,128]{4,3,2,1,0:T(8,128)}, u32[]{:S(2)}) copy-start(f32[1,64,2,8,128]{4,3,2,1,0:T(8,128)} %param.71) | copy-start | bytes 1572868
  1.0 0.7 copy-start.1
  2.1 8.7 %collective-permute-start.92 = (f32[584,128]{1,0:T(8,128)S(1)}, f32[584,128]{1,0:T(8,128)S(1)}, u32[]{:S(2)}, u32[]{:S(2)}) collective-permute-start(f32[584,128]{1,0:T(8,128)S(1)} %get-tuple-element.477), channel_id=1, source_target_pairs={{0,8},{1,9},{2,10},{3,11},{4,12},{5,13},{6,14},{7,15},{8,0},{9,1},... | collective-permute-start | bytes 897032 | tf_op jit(solution)/shard_map/ppermute | solution.py:368
  4.0 8.1 %collective-permute-start.93 = (f32[584,128]{1,0:T(8,128)S(1)}, f32[584,128]{1,0:T(8,128)S(1)}, u32[]{:S(2)}, u32[]{:S(2)}) collective-permute-start(f32[584,128]{1,0:T(8,128)S(1)} %get-tuple-element.478), channel_id=1, source_target_pairs={{0,248},{1,249},{2,250},{3,251},{4,252},{5,253},{6,254},{7,255},{8... | collective-permute-start | bytes 897032 | tf_op jit(solution)/shard_map/ppermute | solution.py:368
  6.2 3.4 %copy-start.6 = (s32[2]{0:T(128)S(1)}, s32[2]{0:T(128)}, u32[]{:S(2)}) copy-start(s32[2]{0:T(128)} %shift_ref.3) | copy-start | bytes 28
  6.2 35.1 %collective-permute-start.94 = (f32[520,128]{1,0:T(8,128)S(1)}, f32[520,128]{1,0:T(8,128)S(1)}, u32[]{:S(2)}, u32[]{:S(2)}) collective-permute-start(f32[520,128]{1,0:T(8,128)S(1)} %get-tuple-element.479), channel_id=1, source_target_pairs={{0,1},{1,0},{2,3},{3,2},{4,5},{5,4},{6,7},{7,6},{8,9},{9,8},{10,11... | collective-permute-start | bytes 798728 | tf_op jit(solution)/shard_map/ppermute | solution.py:368
  8.8 32.4 %collective-permute-start.95 = (f32[520,128]{1,0:T(8,128)S(1)}, f32[520,128]{1,0:T(8,128)S(1)}, u32[]{:S(2)}, u32[]{:S(2)}) collective-permute-start(f32[520,128]{1,0:T(8,128)S(1)} %get-tuple-element.480), channel_id=1, source_target_pairs={{1,2},{2,1},{3,4},{4,3},{5,6},{6,5},{9,10},{10,9},{11,12},{12,11},... | collective-permute-start | bytes 798728 | tf_op jit(solution)/shard_map/ppermute | solution.py:368
  10.8 1.3 %copy-start.7 = (f32[2]{0:T(128)S(1)}, f32[2]{0:T(128)}, u32[]{:S(2)}) copy-start(f32[2]{0:T(128)} %weight_ref.3) | copy-start | bytes 28
  12.8 28.5 %copy-start.2 = (f32[1,3,2,8,128]{4,3,2,1,0:T(8,128)S(1)}, f32[1,3,2,8,128]{4,3,2,1,0:T(8,128)}, u32[]{:S(2)}) copy-start(f32[1,3,2,8,128]{4,3,2,1,0:T(8,128)} %param.72) | copy-start | bytes 73732
  12.8 28.5 %copy-start.3 = (f32[64,64]{1,0:T(8,128)S(1)}, f32[64,64]{1,0:T(8,128)}, u32[]{:S(2)}) copy-start(f32[64,64]{1,0:T(8,128)} %split_ref.3) | copy-start | bytes 49156
  12.8 28.5 %copy-start.4 = (f32[64,64]{1,0:T(8,128)S(1)}, f32[64,64]{1,0:T(8,128)}, u32[]{:S(2)}) copy-start(f32[64,64]{1,0:T(8,128)} %merge_ref.3) | copy-start | bytes 49156
  14.8 11.1 %collective-permute-start.8 = (f32[192,128]{1,0:T(8,128)S(1)}, f32[192,128]{1,0:T(8,128)S(1)}, u32[]{:S(2)}, u32[]{:S(2)}) collective-permute-start(f32[192,128]{1,0:T(8,128)S(1)} %get-tuple-element.334), channel_id=1, source_target_pairs={{7,263},{15,271},{23,279},{31,287},{39,295},{47,303},{55,311},{63,... | collective-permute-start | bytes 294920 | tf_op jit(solution)/shard_map/cond/branch_0_fun/cond/branch_0_fun/cond/branch_1_fun/cond/branch_0_fun/ppermute | solution.py:330
  17.6 19.8 %collective-permute-start.7 = (f32[320,128]{1,0:T(8,128)S(1)}, f32[320,128]{1,0:T(8,128)}, u32[]{:S(2)}, u32[]{:S(2)}) collective-permute-start(f32[320,128]{1,0:T(8,128)S(1)} %get-tuple-element.333), channel_id=1, source_target_pairs={{7,471},{15,479},{23,487},{31,495},{39,503},{47,511},{55,263},{63,... | collective-permute-start | bytes 491528 | tf_op jit(solution)/shard_map/cond/branch_0_fun/cond/branch_0_fun/cond/branch_1_fun/cond/branch_0_fun/ppermute | solution.py:331
  26.0 15.3 %collective-permute-start.9 = (f32[192,128]{1,0:T(8,128)S(1)}, f32[192,128]{1,0:T(8,128)}, u32[]{:S(2)}, u32[]{:S(2)}) collective-permute-start(f32[192,128]{1,0:T(8,128)S(1)} %collective-permute-done.8), channel_id=1, source_target_pairs={{7,55},{15,63},{23,71},{31,79},{39,87},{47,95},{55,103},{63,111},{... | collective-permute-start | bytes 294920 | tf_op jit(solution)/shard_map/cond/branch_0_fun/cond/branch_0_fun/cond/branch_1_fun/cond/branch_0_fun/ppermute | solution.py:332
  41.3 0.7 copy-start.5
  46.0 7.0 %collective-permute-start.96 = (f32[576,128]{1,0:T(8,128)S(1)}, f32[576,128]{1,0:T(8,128)S(1)}, u32[]{:S(2)}, u32[]{:S(2)}) collective-permute-start(f32[576,128]{1,0:T(8,128)S(1)} %get-tuple-element.487), channel_id=1, source_target_pairs={{0,8},{1,9},{2,10},{3,11},{4,12},{5,13},{6,14},{7,15},{8,0},{9,1},... | collective-permute-start | bytes 884744 | tf_op jit(solution)/shard_map/ppermute | solution.py:368
  47.9 8.0 %collective-permute-start.97 = (f32[576,128]{1,0:T(8,128)S(1)}, f32[576,128]{1,0:T(8,128)S(1)}, u32[]{:S(2)}, u32[]{:S(2)}) collective-permute-start(f32[576,128]{1,0:T(8,128)S(1)} %get-tuple-element.488), channel_id=1, source_target_pairs={{0,248},{1,249},{2,250},{3,251},{4,252},{5,253},{6,254},{7,255},{8... | collective-permute-start | bytes 884744 | tf_op jit(solution)/shard_map/ppermute | solution.py:368
  49.8 33.2 %collective-permute-start.98 = (f32[512,128]{1,0:T(8,128)}, f32[512,128]{1,0:T(8,128)S(1)}, u32[]{:S(2)}, u32[]{:S(2)}) collective-permute-start(f32[512,128]{1,0:T(8,128)} %get-tuple-element.489), channel_id=1, source_target_pairs={{0,1},{1,0},{2,3},{3,2},{4,5},{5,4},{6,7},{7,6},{8,9},{9,8},{10,11... | collective-permute-start | bytes 786440 | tf_op jit(solution)/shard_map/ppermute | solution.py:368
  51.7 31.2 %collective-permute-start.99 = (f32[512,128]{1,0:T(8,128)}, f32[512,128]{1,0:T(8,128)S(1)}, u32[]{:S(2)}, u32[]{:S(2)}) collective-permute-start(f32[512,128]{1,0:T(8,128)} %get-tuple-element.490), channel_id=1, source_target_pairs={{1,2},{2,1},{3,4},{4,3},{5,6},{6,5},{9,10},{10,9},{11,12},{12,11},... | collective-permute-start | bytes 786440 | tf_op jit(solution)/shard_map/ppermute | solution.py:368
  58.3 9.1 %collective-permute-start.83 = (f32[192,128]{1,0:T(8,128)S(1)}, f32[192,128]{1,0:T(8,128)S(1)}, u32[]{:S(2)}, u32[]{:S(2)}) collective-permute-start(f32[192,128]{1,0:T(8,128)S(1)} %get-tuple-element.440), channel_id=1, source_target_pairs={{7,263},{15,271},{23,279},{31,287},{39,295},{47,303},{55,311},{63,... | collective-permute-start | bytes 294920 | tf_op jit(solution)/shard_map/cond/branch_1_fun/cond/branch_1_fun/cond/branch_0_fun/cond/branch_0_fun/ppermute | solution.py:330
  63.6 19.3 %collective-permute-start.82 = (f32[320,128]{1,0:T(8,128)S(1)}, f32[320,128]{1,0:T(8,128)}, u32[]{:S(2)}, u32[]{:S(2)}) collective-permute-start(f32[320,128]{1,0:T(8,128)S(1)} %get-tuple-element.439), channel_id=1, source_target_pairs={{7,311},{15,319},{23,327},{31,335},{39,343},{47,351},{55,359},{63,... | collective-permute-start | bytes 491528 | tf_op jit(solution)/shard_map/cond/branch_1_fun/cond/branch_1_fun/cond/branch_0_fun/cond/branch_0_fun/ppermute | solution.py:331
  67.4 15.5 %collective-permute-start.84 = (f32[192,128]{1,0:T(8,128)S(1)}, f32[192,128]{1,0:T(8,128)}, u32[]{:S(2)}, u32[]{:S(2)}) collective-permute-start(f32[192,128]{1,0:T(8,128)S(1)} %collective-permute-done.83), channel_id=1, source_target_pairs={{7,215},{15,223},{23,231},{31,239},{39,247},{47,255},{55,7},{63,15... | collective-permute-start | bytes 294920 | tf_op jit(solution)/shard_map/cond/branch_1_fun/cond/branch_1_fun/cond/branch_0_fun/cond/branch_0_fun/ppermute | solution.py:332

commit v2 on v0

--- a/solution.py
+++ b/solution.py
@@ -8,6 +8,7 @@
 from jax.sharding import PartitionSpec as P
 
 TIME_STEP = 0.2
+GRANT = 8 * 1024 * 1024
 AXES = ("region", "sector", "block")
 SECTIONS = 64
 CELLS = 8
@@ -15,6 +16,8 @@
 AXIAL = 128
 ROW_BYTES_ROWS = CELLS * SECTIONS
 STRIDE = ROWS * CELLS
+PARTS = 4
+PART = SECTIONS // PARTS
 OWN = 40
 CROSS = SECTIONS - OWN
 DIRECT_CHIPS = 1
@@ -35,15 +38,16 @@
     ]
 
 
-def block_pairs(step):
+def block_pairs(first):
     count = lax.axis_size("block")
-    return [
-        (device_number(r, s, b), device_number(r, s, b + step))
-        for r in range(2)
-        for s in range(lax.axis_size("sector"))
-        for b in range(count)
-        if 0 <= b + step < count
-    ]
+    pairs = []
+    for r in range(2):
+        for s in range(lax.axis_size("sector")):
+            for b in range(count):
+                to = b + 1 if b % 2 == first else b - 1
+                if 0 <= to < count:
+                    pairs.append((device_number(r, s, b), device_number(r, s, to)))
+    return pairs
 
 
 def turn_pairs(sectors, across):
@@ -63,28 +67,64 @@
     return pl.ds(index * SECTIONS, SECTIONS)
 
 
-def pack_kernel(field_ref, speed_ref, up_ref, down_ref, next_ref, prev_ref):
-    for row, out_ref in ((0, down_ref), (1, up_ref)):
+def is_even(axis):
+    return lax.axis_index(axis) % 2 == 0
+
+
+def pack_kernel(
+    shift_ref,
+    field_hbm,
+    speed_hbm,
+    low_ref,
+    high_ref,
+    first_block_ref,
+    second_block_ref,
+    next_ref,
+    prev_ref,
+    first_chips_ref,
+    second_chips_ref,
+    field_ref,
+    speed_ref,
+    sems,
+):
+    copies = [pltpu.make_async_copy(speed_hbm, speed_ref, sems.at[PARTS])]
+    for part in range(PARTS):
+        where = pl.ds(part * PART * STRIDE, PART * STRIDE)
+        copies.append(pltpu.make_async_copy(field_hbm.at[where, :], field_ref.at[where, :], sems.at[part]))
+    for copy in copies:
+        copy.start()
+    for substep, chips_ref in enumerate((first_chips_ref, second_chips_ref)):
+        chips = (shift_ref[substep] + CELLS) // STRIDE % (lax.axis_size("sector") // 2)
+        chips_ref[...] = jnp.full((1, 1), chips, jnp.int32)
+    up_is_first = is_even("block")
+    for part in range(PARTS):
+        copies[1 + part].wait()
         for a in range(CELLS):
-            cells = field_ref[pl.ds(row * CELLS + a, SECTIONS, stride=STRIDE), :]
-            store_cells(row, a, cells, up_ref, down_ref, next_ref, prev_ref)
-        out_ref[pl.ds(ROW_BYTES_ROWS, CELLS), :] = speed_ref[pl.ds(STRIDE + row * CELLS, CELLS), :]
+            low, high = [
+                field_ref[pl.ds(part * PART * STRIDE + row * CELLS + a, PART, stride=STRIDE), :] for row in range(ROWS)
+            ]
+            store_cells(pl.ds(a * SECTIONS + part * PART, PART), low, high, up_is_first, low_ref, high_ref, first_block_ref, second_block_ref, next_ref, prev_ref)
+            if a in (0, CELLS - 1):
+                edge_ref = next_ref if a else prev_ref
+                edge_ref[pl.ds(ROW_BYTES_ROWS + part * PART, PART), :] = low
+    copies[0].wait()
+    low, high = [speed_ref[pl.ds(STRIDE + row * CELLS, CELLS), :] for row in range(ROWS)]
+    first_block_ref[pl.ds(ROW_BYTES_ROWS, CELLS), :] = jnp.where(up_is_first, high, low)
+    second_block_ref[pl.ds(ROW_BYTES_ROWS, CELLS), :] = jnp.where(up_is_first, low, high)
     for edge_ref, a in ((prev_ref, 0), (next_ref, CELLS - 1)):
         edge_ref[pl.ds(EDGE, 8), :] = jnp.zeros((8, AXIAL), jnp.float32)
         for row in range(ROWS):
             edge_ref[pl.ds(EDGE + row, 1), :] = speed_ref[pl.ds(row * CELLS + a, 1), :]
 
 
-def store_cells(row, a, cells, up_ref, down_ref, next_ref, prev_ref):
-    if row == ROWS - 1:
-        for out_ref in (up_ref, next_ref, prev_ref):
-            out_ref[line(a), :] = cells
-    else:
-        down_ref[line(a), :] = cells
-        if a == 0:
-            prev_ref[line(CELLS), :] = cells
-        if a == CELLS - 1:
-            next_ref[line(CELLS), :] = cells
+def store_cells(
+    where, low, high, up_is_first, low_ref, high_ref, first_block_ref, second_block_ref, next_ref, prev_ref
+):
+    low_ref[where, :] = low
+    first_block_ref[where, :] = jnp.where(up_is_first, high, low)
+    second_block_ref[where, :] = jnp.where(up_is_first, low, high)
+    for out_ref in (high_ref, next_ref, prev_ref):
+        out_ref[where, :] = high
 
 
 def lines(count):
@@ -95,16 +135,25 @@
     return [pl.BlockSpec(memory_space=pltpu.VMEM)] * count
 
 
-def pack(field, speeds):
+def pack(shifts, field, speeds):
+    row = lines(ROW_BYTES_ROWS)
     rim = lines(ROW_BYTES_ROWS + CELLS)
     edge = lines(EDGE + 8)
+    number = jax.ShapeDtypeStruct((1, 1), jnp.int32)
+    smem = pl.BlockSpec(memory_space=pltpu.SMEM)
     return pl.pallas_call(
         pack_kernel,
-        out_shape=(rim, rim, edge, edge),
-        in_specs=vmem(2),
-        out_specs=tuple(vmem(4)),
+        out_shape=(row, row, rim, rim, edge, edge, number, number),
+        in_specs=[smem] + [pl.BlockSpec(memory_space=pltpu.HBM)] * 2,
+        out_specs=tuple(vmem(8)),
+        scratch_shapes=[
+            pltpu.VMEM(field.shape, jnp.float32),
+            pltpu.VMEM(speeds.shape, jnp.float32),
+            pltpu.SemaphoreType.DMA((PARTS + 1,)),
+        ],
+        compiler_params=pltpu.CompilerParams(vmem_limit_bytes=GRANT),
         name="pack",
-    )(field, speeds)
+    )(shifts, field, speeds)
 
 
 def align_kernel(substep, shift_ref, weight_ref, own_ref, prev_ref, next_ref, direct_ref, cross_ref, row_ref):
@@ -134,6 +183,7 @@
         in_specs=[pl.BlockSpec(memory_space=pltpu.SMEM)] * 2 + vmem(3),
         out_specs=tuple(vmem(2)),
         scratch_shapes=[pltpu.VMEM((3 * ROW_BYTES_ROWS, AXIAL), jnp.float32)],
+        compiler_params=pltpu.CompilerParams(vmem_limit_bytes=GRANT),
         name="align",
     )(shifts, weights, own, from_prev, from_next)
 
@@ -146,18 +196,18 @@
 
 def substep_kernel(
     final,
-    up_ref,
-    down_ref,
+    low_ref,
+    high_ref,
     prev_ref,
     next_ref,
-    below_ref,
-    above_ref,
-    direct_ref,
-    cross_ref,
+    first_block_ref,
+    second_block_ref,
+    direct_any,
+    cross_any,
     prev_rim_ref,
     next_rim_ref,
-    below_rim_ref,
-    above_rim_ref,
+    first_block_rim_ref,
+    second_block_rim_ref,
     speed_ref,
     strain_ref,
     split_ref,
@@ -165,24 +215,26 @@
     *refs,
 ):
     if final:
-        out_ref, coef_ref, top_ref = refs
+        out_any, out_ref, *scratch = refs
     else:
-        *new_refs, coef_ref, top_ref = refs
+        new_refs, scratch = refs[:6], refs[6:]
+    coef_ref, top_ref, direct_ref, cross_ref, sems = scratch
+    arrivals = [
+        pltpu.make_async_copy(direct_any, direct_ref, sems.at[0]),
+        pltpu.make_async_copy(cross_any, cross_ref, sems.at[1]),
+    ]
+    for copy in arrivals:
+        copy.start()
     block = lax.axis_index("block")
     first_block = block == 0
     last_block = block == lax.axis_size("block") - 1
-    below_speed = below_rim_ref[pl.ds(ROW_BYTES_ROWS, CELLS), :]
-    above_speed = above_rim_ref[pl.ds(ROW_BYTES_ROWS, CELLS), :]
-
-    @pl.when(last_block)
-    def _():
-        for a in range(CELLS):
-            top_ref[pl.ds(a * SECTIONS, OWN), :] = direct_ref[pl.ds(a * OWN, OWN), :]
-            top_ref[pl.ds(a * SECTIONS + OWN, CROSS), :] = cross_ref[pl.ds(a * CROSS, CROSS), :]
-
-    @pl.when(jnp.logical_not(last_block))
-    def _():
-        top_ref[...] = above_ref[pl.ds(0, ROW_BYTES_ROWS), :]
+    up_is_first = is_even("block")
+
+    def by_block(lines_of, first_ref=first_block_ref, second_ref=second_block_ref):
+        one, two = first_ref[lines_of, :], second_ref[lines_of, :]
+        return jnp.where(up_is_first, one, two), jnp.where(up_is_first, two, one)
+
+    above_speed, below_speed = by_block(pl.ds(ROW_BYTES_ROWS, CELLS), first_block_rim_ref, second_block_rim_ref)
 
     for row in range(ROWS):
         azim = speed_ref[pl.ds(row * CELLS, CELLS), :]
@@ -219,8 +271,24 @@
     both_low = jnp.concatenate([split_low, merge_low], axis=0)
     left = jnp.concatenate([both_high, both_high, both_low], axis=1)
 
+    leaves = []
     for row in range(ROWS):
-        own_ref = (down_ref, up_ref)[row]
+        own_ref = (low_ref, high_ref)[row]
+        if row == ROWS - 1:
+            for copy in arrivals:
+                copy.wait()
+
+            @pl.when(last_block)
+            def _():
+                for a in range(CELLS):
+                    top_ref[pl.ds(a * SECTIONS, OWN), :] = direct_ref[pl.ds(a * OWN, OWN), :]
+                    top_ref[pl.ds(a * SECTIONS + OWN, CROSS), :] = cross_ref[pl.ds(a * CROSS, CROSS), :]
+
+            @pl.when(jnp.logical_not(last_block))
+            def _():
+                for a in range(CELLS):
+                    top_ref[line(a), :] = by_block(line(a))[0]
+
         for pair in range(CELLS // 2):
             cells_of = [own_ref[line(2 * pair + i), :] for i in range(2)]
             wide = jnp.concatenate(cells_of, axis=1)
@@ -234,9 +302,9 @@
                 joined = products[SECTIONS:, i * AXIAL : (i + 1) * AXIAL]
                 coef = lambda n: coef_ref[n, pl.ds(row * CELLS + a, 1), :]
                 if row == 0:
-                    outer, inner = up_ref[line(a), :], below_ref[line(a), :]
+                    outer, inner = high_ref[line(a), :], by_block(line(a))[1]
                 else:
-                    outer, inner = top_ref[line(a), :], down_ref[line(a), :]
+                    outer, inner = top_ref[line(a), :], low_ref[line(a), :]
                 later = next_ref[line(0 if row else CELLS), :] if a == CELLS - 1 else own_ref[line(a + 1), :]
                 earlier = prev_ref[line(CELLS - 1 if row else CELLS), :] if a == 0 else own_ref[line(a - 1), :]
                 value = cells * (coef(6) + joined)
@@ -247,44 +315,64 @@
                     coef(4) * pltpu.roll(cells, AXIAL - 1, 1) + coef(5) * pltpu.roll(cells, 1, 1)
                 )
                 if final:
-                    out_ref[pl.ds(row * CELLS + a, SECTIONS, stride=STRIDE), :] = value
+                    out_lines = out_ref.reshape(SECTIONS * STRIDE, AXIAL)
+                    out_lines[pl.ds(row * CELLS + a, SECTIONS, stride=STRIDE), :] = value
+                elif row == 0:
+                    new_refs[0][line(a), :] = value
+                    if a in (0, CELLS - 1):
+                        edge_ref = new_refs[4] if a else new_refs[5]
+                        edge_ref[line(CELLS), :] = value
                 else:
-                    store_cells(row, a, value, *new_refs)
+                    store_cells(line(a), new_refs[0][line(a), :], value, up_is_first, *new_refs)
+        if final:
+            rows = pl.ds(row * CELLS, CELLS)
+            leave = pltpu.make_async_copy(out_ref.at[:, rows, :], out_any.at[:, rows, :], sems.at[2 + row])
+            leave.start()
+            leaves.append(leave)
+    for leave in leaves:
+        leave.wait()
 
 
 def run_substep(final, *arrays):
+    scratch = [
+        pltpu.VMEM((8, STRIDE, AXIAL), jnp.float32),
+        pltpu.VMEM((ROW_BYTES_ROWS, AXIAL), jnp.float32),
+        pltpu.VMEM((CELLS * OWN, AXIAL), jnp.float32),
+        pltpu.VMEM((CELLS * CROSS, AXIAL), jnp.float32),
+        pltpu.SemaphoreType.DMA((2 + ROWS,)),
+    ]
     if final:
-        out_shape, out_specs = lines(SECTIONS * STRIDE), vmem(1)[0]
+        out_shape = jax.ShapeDtypeStruct((SECTIONS, STRIDE, AXIAL), jnp.float32)
+        out_specs = pl.BlockSpec(memory_space=pltpu.HBM)
+        scratch.insert(0, pltpu.VMEM(out_shape.shape, jnp.float32))
     else:
-        out_shape = (lines(ROW_BYTES_ROWS), lines(ROW_BYTES_ROWS), lines(EDGE), lines(EDGE))
-        out_specs = tuple(vmem(4))
+        out_shape = (lines(ROW_BYTES_ROWS),) * 4 + (lines(EDGE),) * 2
+        out_specs = tuple(vmem(6))
+    in_specs = vmem(len(arrays))
+    in_specs[6:8] = [pl.BlockSpec(memory_space=pl.ANY)] * 2
     return pl.pallas_call(
         functools.partial(substep_kernel, final),
         out_shape=out_shape,
-        in_specs=vmem(len(arrays)),
+        in_specs=in_specs,
         out_specs=out_specs,
-        scratch_shapes=[
-            pltpu.VMEM((8, STRIDE, AXIAL), jnp.float32),
-            pltpu.VMEM((ROW_BYTES_ROWS, AXIAL), jnp.float32),
-        ],
-        compiler_params=pltpu.CompilerParams(vmem_limit_bytes=32 * 1024 * 1024),
+        scratch_shapes=scratch,
+        compiler_params=pltpu.CompilerParams(vmem_limit_bytes=GRANT),
         name="substep",
     )(*arrays)
 
 
-def turned(shift, direct, cross):
+def turned(chips, direct, cross):
     count = lax.axis_size("sector") // 2
 
-    def turn(chips, direct, cross):
-        chips = chips % count
-        distance = min(chips, count - chips)
+    def turn(steps, direct, cross):
+        distance = min(steps, count - steps)
         if distance <= DIRECT_CHIPS or 2 * distance == count:
-            cross = lax.ppermute(cross, AXES, turn_pairs(2 * chips, True))
-            direct = lax.ppermute(direct, AXES, turn_pairs(2 * chips, True))
+            cross = lax.ppermute(cross, AXES, turn_pairs(2 * steps, True))
+            direct = lax.ppermute(direct, AXES, turn_pairs(2 * steps, True))
         else:
             cross = lax.ppermute(cross, AXES, turn_pairs(0, True))
-            direct = lax.ppermute(direct, AXES, turn_pairs(2 * chips, True))
-            cross = lax.ppermute(cross, AXES, turn_pairs(2 * chips, False))
+            direct = lax.ppermute(direct, AXES, turn_pairs(2 * steps, True))
+            cross = lax.ppermute(cross, AXES, turn_pairs(2 * steps, False))
         return direct, cross
 
     def choose(low, high, direct, cross):
@@ -292,14 +380,14 @@
             return turn(low, direct, cross)
         middle = (low + high) // 2
         return lax.cond(
-            shift < middle * STRIDE - CELLS,
+            chips < middle,
             functools.partial(choose, low, middle),
             functools.partial(choose, middle, high),
             direct,
             cross,
         )
 
-    return choose(0, count + 1, direct, cross)
+    return choose(0, count, direct, cross)
 
 
 def body(
@@ -315,22 +403,22 @@
     speeds = frame_motion_vector.reshape(3 * STRIDE, AXIAL)
     strain = strain_factor.reshape(STRIDE, AXIAL)
     shifts, weights = spinning_shift_history, nearest_coverage_fraction
-    arrays = pack(field, speeds)
+    *arrays, first_chips, second_chips = pack(shifts, field, speeds)
     rims = None
-    for substep in range(2):
-        up, down, to_next, to_prev = arrays
+    for substep, chips in enumerate((first_chips, second_chips)):
+        low, high, first, second, to_next, to_prev = arrays
         from_prev = lax.ppermute(to_next, AXES, sector_pairs(1))
         from_next = lax.ppermute(to_prev, AXES, sector_pairs(-1))
-        below = lax.ppermute(up, AXES, block_pairs(1))
-        above = lax.ppermute(down, AXES, block_pairs(-1))
-        direct, cross = align(substep, shifts, weights, up, from_prev, from_next)
-        direct, cross = turned(shifts[substep], direct, cross)
-        halos = (from_prev, from_next, below, above)
+        first = lax.ppermute(first, AXES, block_pairs(0))
+        second = lax.ppermute(second, AXES, block_pairs(1))
+        direct, cross = align(substep, shifts, weights, high, from_prev, from_next)
+        direct, cross = turned(chips[0, 0], direct, cross)
+        halos = (from_prev, from_next, first, second)
         rims = rims or halos
         arrays = run_substep(
             substep == 1,
-            up,
-            down,
+            low,
+            high,
             *halos,
             direct,
             cross,

time: 111 us -> 106 us (0.955)
  starting transfers between devices: 55.3 us -> 48.9 us
  waiting for transfers between devices: 34.4 us -> 39.8 us
  local copies, waits for them, and re-layouts: 7.25 us -> 3.32 us
    ppermute x8, starting transfers between devices: 38.7 us -> 31.4 us  [the longest x2 19.2 us: turn(): direct = lax.ppermute(direct, AXES, turn_pairs(2 * steps, True))]
    ppermute x8, waiting for transfers between devices: 34.4 us -> 38.1 us  [the longest x2 36.1 us: turn(): direct = lax.ppermute(direct, AXES, turn_pairs(2 * steps, True))]
    unnamed x36 -> x16, local copies, waits for them, and re-layouts: 6.68 us -> 3.32 us
    ppermute x2, waiting for transfers between devices: 0.01 us -> 1.67 us  [body(): from_prev = lax.ppermute(to_next, AXES, sector_pairs(1))]
    pallas_call x2, Pallas kernels: 2.52 us -> 1.27 us  [align(): pl.pallas_call(functools.partial(align_kernel, substep), out_shape=(lines...]
  transfers between devices with their start and end apart: 14 -> 14, of which waited for: 3 -> 5; matrix products, arithmetic and copies ran while one was open for 1% -> 0% of each run, Pallas kernels for 2% -> 1%
where the time goes in v2:
time: 106 us; the launch traced here: 105 us
  starting transfers between devices  48.9 us (46%)
  waiting for transfers between devices  39.8 us (38%)
  Pallas kernels  7.71 us (7%)
  loops' own time  3.8 us (4%)
  local copies, waits for them, and re-layouts  3.32 us (3%)
  between operations  1.36 us (1%)
    ppermute x2, waiting for transfers between devices, turn(): direct = lax.ppermute(direct, AXES, turn_pairs(2 * steps, True))  36.1 us
    ppermute x2, starting transfers between devices, turn(): direct = lax.ppermute(direct, AXES, turn_pairs(2 * steps, True))  19.2 us
    ppermute x2, starting transfers between devices, body(): from_next = lax.ppermute(to_prev, AXES, sector_pairs(-1))  11.8 us
    ppermute x2, starting transfers between devices, turn(): cross = lax.ppermute(cross, AXES, turn_pairs(2 * steps, False))  6.3 us
    ppermute x2, starting transfers between devices, turn(): cross = lax.ppermute(cross, AXES, turn_pairs(0, True))  5.57 us
    ppermute x2, starting transfers between devices, body(): first = lax.ppermute(first, AXES, block_pairs(0))  4.55 us
    pallas_call x2, Pallas kernels, run_substep(): pl.pallas_call(functools.partial(substep_kernel, final), out_shape=out_sh...  4.41 us
    another operation x8, loops' own time, choose(): lax.cond(chips < middle, functools.partial(choose, low, middle), functool...  3.8 us
  transfers between devices with their start and end apart: 14, of which 5 were waited for; matrix products, arithmetic and copies ran while one was open for 0% of the time, Pallas kernels for 1%

profile of v2, /device:TPU:30, one launch (start us, length us, event | category | flops | bytes accessed | tf_op | source)
XLA Modules:
  0.0 104.9 jit_solution(16928704653520873426)
XLA Ops:
  0.0 0.7 copy-done.6
  0.7 1.0 copy-done
  1.7 0.7 copy-done.1
  2.4 2.0 %pack.1 = (f32[512,128]{1,0:T(8,128)S(1)}, f32[512,128]{1,0:T(8,128)S(1)}, f32[520,128]{1,0:T(8,128)S(1)}, f32[520,128]{1,0:T(8,128)S(1)}, f32[584,128]{1,0:T(8,...) custom-call(s32[2]{0:T(128)S(1)} %copy-done.6, f32[1024,128]{1,0:T(8,128)S(1)} %bitcast.6, ...), custom_call_target="tpu_custom_call" | custom-call | tf_op jit(solution)/shard_map/pack/pallas_call | solution.py:144
  4.5 8.9 %collective-permute-start.89 = (f32[584,128]{1,0:T(8,128)S(1)}, f32[584,128]{1,0:T(8,128)S(1)}, u32[]{:S(2)}, u32[]{:S(2)}) collective-permute-start(f32[584,128]{1,0:T(8,128)S(1)} %get-tuple-element.450), channel_id=1, source_target_pairs={{0,248},{1,249},{2,250},{3,251},{4,252},{5,253},{6,254},{7,255},{8... | collective-permute-start | bytes 897032 | tf_op jit(solution)/shard_map/ppermute | solution.py:411
  13.4 2.6 %collective-permute-start.90 = (f32[520,128]{1,0:T(8,128)S(1)}, f32[520,128]{1,0:T(8,128)S(1)}, u32[]{:S(2)}, u32[]{:S(2)}) collective-permute-start(f32[520,128]{1,0:T(8,128)S(1)} %get-tuple-element.451), channel_id=1, source_target_pairs={{0,1},{1,0},{2,3},{3,2},{4,5},{5,4},{6,7},{7,6},{8,9},{9,8},{10,11... | collective-permute-start | bytes 798728 | tf_op jit(solution)/shard_map/ppermute | solution.py:412
  16.1 0.7 collective-permute-start.91
  18.8 38.5 %conditional.30 = ((f32[320,128]{1,0:T(8,128)}, f32[192,128]{1,0:T(8,128)})) conditional(s32[]{:T(128)} %convert_element_type.90, (s32[]{:T(128)}, f32[320,128]{1,0:T(8,128)S(1)}, f32[192,128]{1,0:T(8,128)S(1)}) %tuple.193, (s32[]{:T(128)}, f32[320,128]{1,0:T(8,128)S(1)}, f32[192,128]{1,0:T(8,128)S(1)}) %tuple.193), branch_computations={%region_0.0_spmd, %region_15.0_spmd} | conditional | flops 6 | bytes 1441994 | solution.py:382
  19.4 37.8 %conditional.13 = ((f32[320,128]{1,0:T(8,128)}, f32[192,128]{1,0:T(8,128)})) conditional(s32[]{:T(128)} %convert_element_type.73, (s32[]{:T(128)}, f32[320,128]{1,0:T(8,128)S(1)}, f32[192,128]{1,0:T(8,128)S(1)}) %param.29, (s32[]{:T(128)}, f32[320,128]{1,0:T(8,128)S(1)}, f32[192,128]{1,0:T(8,128)S(1)}) %param.29), branch_computations={%region_16.0_spmd, %region_23.0_spmd} | conditional | flops 4 | bytes 1441980 | solution.py:382
  20.1 37.1 %conditional.9 = ((f32[320,128]{1,0:T(8,128)}, f32[192,128]{1,0:T(8,128)})) conditional(s32[]{:T(128)} %convert_element_type.69, (s32[]{:T(128)}, f32[320,128]{1,0:T(8,128)S(1)}, f32[192,128]{1,0:T(8,128)S(1)}) %param.21, (s32[]{:T(128)}, f32[320,128]{1,0:T(8,128)S(1)}, f32[192,128]{1,0:T(8,128)S(1)}) %param.21), branch_computations={%region_17.0_spmd, %region_20.0_spmd} | conditional | flops 2 | bytes 1441966 | solution.py:382
  20.8 36.5 %conditional.7 = (f32[320,128]{1,0:T(8,128)}, f32[192,128]{1,0:T(8,128)}) conditional(s32[]{:T(128)} %convert_element_type.67, (f32[320,128]{1,0:T(8,128)S(1)}, f32[192,128]{1,0:T(8,128)S(1)}) %tuple.143, (f32[320,128]{1,0:T(8,128)S(1)}, f32[192,128]{1,0:T(8,128)S(1)}) %tuple.143), branch_computations={%region_18.0_spmd, %region_19.0_spmd} | conditional | bytes 1441928 | solution.py:382
  20.8 2.7 %collective-permute-start.23 = (f32[192,128]{1,0:T(8,128)S(1)}, f32[192,128]{1,0:T(8,128)S(1)}, u32[]{:S(2)}, u32[]{:S(2)}) collective-permute-start(f32[192,128]{1,0:T(8,128)S(1)} %get-tuple-element.333), channel_id=1, source_target_pairs={{7,263},{15,271},{23,279},{31,287},{39,295},{47,303},{55,311},{63,... | collective-permute-start | bytes 294920 | tf_op jit(solution)/shard_map/cond/branch_1_fun/cond/branch_0_fun/cond/branch_0_fun/cond/branch_0_fun/ppermute | solution.py:373
  23.5 8.7 %collective-permute-start.22 = (f32[320,128]{1,0:T(8,128)S(1)}, f32[320,128]{1,0:T(8,128)}, u32[]{:S(2)}, u32[]{:S(2)}) collective-permute-start(f32[320,128]{1,0:T(8,128)S(1)} %get-tuple-element.332), channel_id=1, source_target_pairs={{7,375},{15,383},{23,391},{31,399},{39,407},{47,415},{55,423},{63,... | collective-permute-start | bytes 491528 | tf_op jit(solution)/shard_map/cond/branch_1_fun/cond/branch_0_fun/cond/branch_0_fun/cond/branch_0_fun/ppermute | solution.py:374
  32.2 4.4 %collective-permute-start.24 = (f32[192,128]{1,0:T(8,128)S(1)}, f32[192,128]{1,0:T(8,128)}, u32[]{:S(2)}, u32[]{:S(2)}) collective-permute-start(f32[192,128]{1,0:T(8,128)S(1)} %collective-permute-done.23), channel_id=1, source_target_pairs={{7,151},{15,159},{23,167},{31,175},{39,183},{47,191},{55,199},{63,... | collective-permute-start | bytes 294920 | tf_op jit(solution)/shard_map/cond/branch_1_fun/cond/branch_0_fun/cond/branch_0_fun/cond/branch_0_fun/ppermute | solution.py:375
  36.6 18.6 %collective-permute-done.22 = f32[320,128]{1,0:T(8,128)} collective-permute-done((f32[320,128]{1,0:T(8,128)S(1)}, f32[320,128]{1,0:T(8,128)}, u32[]{:S(2)}, u32[]{:S(2)}) %collective-permute-start.22) | collective-permute-done | bytes 163872 | tf_op jit(solution)/shard_map/cond/branch_1_fun/cond/branch_0_fun/cond/branch_0_fun/cond/branch_0_fun/ppermute | solution.py:374
  55.2 2.0 %collective-permute-done.24 = f32[192,128]{1,0:T(8,128)} collective-permute-done((f32[192,128]{1,0:T(8,128)S(1)}, f32[192,128]{1,0:T(8,128)}, u32[]{:S(2)}, u32[]{:S(2)}) %collective-permute-start.24) | collective-permute-done | bytes 98336 | tf_op jit(solution)/shard_map/cond/branch_1_fun/cond/branch_0_fun/cond/branch_0_fun/cond/branch_0_fun/ppermute | solution.py:375
  57.3 0.7 copy-done.5
  57.9 2.3 %substep.2 = (f32[512,128]{1,0:T(8,128)S(1)}, f32[512,128]{1,0:T(8,128)S(1)}, f32[512,128]{1,0:T(8,128)}, f32[512,128]{1,0:T(8,128)}, f32[576,128]{1,0:T(8,128)S(1)}, /*index=5*/f32[576,128]{1,0:T(8,128)S(1)}) custom-call(f32[512,128]{1,0:T(8,128)S(1)} %get-tuple-element.447.low_ref, f32[512,128]{1,0:T(8,128)S(1)} %get-tuple-element.448.own_ref.high_ref, ...), custom_call_target="tpu_custom_call" | custom-call | tf_op jit(solution)/shard_map/substep/pallas_call | solution.py:353
  60.3 2.9 %collective-permute-start.93 = (f32[576,128]{1,0:T(8,128)S(1)}, f32[576,128]{1,0:T(8,128)S(1)}, u32[]{:S(2)}, u32[]{:S(2)}) collective-permute-start(f32[576,128]{1,0:T(8,128)S(1)} %get-tuple-element.461), channel_id=1, source_target_pairs={{0,248},{1,249},{2,250},{3,251},{4,252},{5,253},{6,254},{7,255},{8... | collective-permute-start | bytes 884744 | tf_op jit(solution)/shard_map/ppermute | solution.py:411
  63.2 1.9 %collective-permute-start.94 = (f32[512,128]{1,0:T(8,128)}, f32[512,128]{1,0:T(8,128)S(1)}, u32[]{:S(2)}, u32[]{:S(2)}) collective-permute-start(f32[512,128]{1,0:T(8,128)} %get-tuple-element.462), channel_id=1, source_target_pairs={{0,1},{1,0},{2,3},{3,2},{4,5},{5,4},{6,7},{7,6},{8,9},{9,8},{10,11... | collective-permute-start | bytes 786440 | tf_op jit(solution)/shard_map/ppermute | solution.py:412
  65.1 0.7 collective-permute-start.95
  66.3 1.2 %collective-permute-done.92.prev_ref = f32[576,128]{1,0:T(8,128)S(1)} collective-permute-done((f32[576,128]{1,0:T(8,128)S(1)}, f32[576,128]{1,0:T(8,128)S(1)}, u32[]{:S(2)}, u32[]{:S(2)}) %collective-permute-start.92) | collective-permute-done | bytes 294944 | tf_op jit(solution)/shard_map/ppermute | solution.py:410
  67.6 0.6 align.3
  68.2 34.6 %conditional.31 = ((f32[320,128]{1,0:T(8,128)}, f32[192,128]{1,0:T(8,128)})) conditional(s32[]{:T(128)} %convert_element_type.91, (s32[]{:T(128)}, f32[320,128]{1,0:T(8,128)S(1)}, f32[192,128]{1,0:T(8,128)S(1)}) %tuple.194, (s32[]{:T(128)}, f32[320,128]{1,0:T(8,128)S(1)}, f32[192,128]{1,0:T(8,128)S(1)}) %tuple.194), branch_computations={%region_30.0_spmd, %region_45.0_spmd} | conditional | flops 6 | bytes 1441994 | solution.py:382
  68.8 34.0 %conditional.27 = ((f32[320,128]{1,0:T(8,128)}, f32[192,128]{1,0:T(8,128)})) conditional(s32[]{:T(128)} %convert_element_type.87, (s32[]{:T(128)}, f32[320,128]{1,0:T(8,128)S(1)}, f32[192,128]{1,0:T(8,128)S(1)}) %param.59, (s32[]{:T(128)}, f32[320,128]{1,0:T(8,128)S(1)}, f32[192,128]{1,0:T(8,128)S(1)}) %param.59), branch_computations={%region_46.0_spmd, %region_53.0_spmd} | conditional | flops 4 | bytes 1441980 | solution.py:382
  69.4 33.4 %conditional.23 = ((f32[320,128]{1,0:T(8,128)}, f32[192,128]{1,0:T(8,128)})) conditional(s32[]{:T(128)} %convert_element_type.83, (s32[]{:T(128)}, f32[320,128]{1,0:T(8,128)S(1)}, f32[192,128]{1,0:T(8,128)S(1)}) %param.51, (s32[]{:T(128)}, f32[320,128]{1,0:T(8,128)S(1)}, f32[192,128]{1,0:T(8,128)S(1)}) %param.51), branch_computations={%region_47.0_spmd, %region_50.0_spmd} | conditional | flops 2 | bytes 1441966 | solution.py:382
  69.9 32.8 %conditional.22 = (f32[320,128]{1,0:T(8,128)}, f32[192,128]{1,0:T(8,128)}) conditional(s32[]{:T(128)} %convert_element_type.82, (f32[320,128]{1,0:T(8,128)S(1)}, f32[192,128]{1,0:T(8,128)S(1)}) %tuple.179, (f32[320,128]{1,0:T(8,128)S(1)}, f32[192,128]{1,0:T(8,128)S(1)}) %tuple.179), branch_computations={%region_51.0_spmd, %region_52.0_spmd} | conditional | bytes 1441928 | solution.py:382
  69.9 2.8 %collective-permute-start.73 = (f32[192,128]{1,0:T(8,128)S(1)}, f32[192,128]{1,0:T(8,128)S(1)}, u32[]{:S(2)}, u32[]{:S(2)}) collective-permute-start(f32[192,128]{1,0:T(8,128)S(1)} %get-tuple-element.402), channel_id=1, source_target_pairs={{7,263},{15,271},{23,279},{31,287},{39,295},{47,303},{55,311},{63,... | collective-permute-start | bytes 294920 | tf_op jit(solution)/shard_map/cond/branch_1_fun/cond/branch_0_fun/cond/branch_1_fun/cond/branch_0_fun/ppermute | solution.py:373
  72.8 10.5 %collective-permute-start.72 = (f32[320,128]{1,0:T(8,128)S(1)}, f32[320,128]{1,0:T(8,128)}, u32[]{:S(2)}, u32[]{:S(2)}) collective-permute-start(f32[320,128]{1,0:T(8,128)S(1)} %get-tuple-element.401), channel_id=1, source_target_pairs={{7,343},{15,351},{23,359},{31,367},{39,375},{47,383},{55,391},{63,... | collective-permute-start | bytes 491528 | tf_op jit(solution)/shard_map/cond/branch_1_fun/cond/branch_0_fun/cond/branch_1_fun/cond/branch_0_fun/ppermute | solution.py:374
  83.3 1.9 %collective-permute-start.74 = (f32[192,128]{1,0:T(8,128)S(1)}, f32[192,128]{1,0:T(8,128)}, u32[]{:S(2)}, u32[]{:S(2)}) collective-permute-start(f32[192,128]{1,0:T(8,128)S(1)} %collective-permute-done.73), channel_id=1, source_target_pairs={{7,183},{15,191},{23,199},{31,207},{39,215},{47,223},{55,231},{63,... | collective-permute-start | bytes 294920 | tf_op jit(solution)/shard_map/cond/branch_1_fun/cond/branch_0_fun/cond/branch_1_fun/cond/branch_0_fun/ppermute | solution.py:375
  85.2 17.5 %collective-permute-done.72 = f32[320,128]{1,0:T(8,128)} collective-permute-done((f32[320,128]{1,0:T(8,128)S(1)}, f32[320,128]{1,0:T(8,128)}, u32[]{:S(2)}, u32[]{:S(2)}) %collective-permute-start.72) | collective-permute-done | bytes 163872 | tf_op jit(solution)/shard_map/cond/branch_1_fun/cond/branch_0_fun/cond/branch_1_fun/cond/branch_0_fun/ppermute | solution.py:374
  102.8 2.1 %substep.3 = f32[64,16,128]{2,1,0:T(8,128)} custom-call(f32[512,128]{1,0:T(8,128)S(1)} %get-tuple-element.458.low_ref, f32[512,128]{1,0:T(8,128)S(1)} %get-tuple-element.459.own_ref.high_ref, f32[576,128]{1,0:T(8,128)S(1)} %collective-permute-done.92.prev_ref, f32[576,128]{1,0:T(8,128)S(1)} %collective-permute-done.93.next_ref, ...), custom_call_target="tpu_custom_call" | custom-call | tf_op jit(solution)/shard_map/substep/pallas_call | solution.py:353
  (25 shorter events, 1.4 us)
Async XLA Ops:
  0.0 0.7 copy-start.6
  0.7 1.0 copy-start
  1.7 0.7 copy-start.1
  4.5 13.4 %collective-permute-start.88 = (f32[584,128]{1,0:T(8,128)S(1)}, f32[584,128]{1,0:T(8,128)S(1)}, u32[]{:S(2)}, u32[]{:S(2)}) collective-permute-start(f32[584,128]{1,0:T(8,128)S(1)} %get-tuple-element.449), channel_id=1, source_target_pairs={{0,8},{1,9},{2,10},{3,11},{4,12},{5,13},{6,14},{7,15},{8,16},{9,17... | collective-permute-start | bytes 897032 | tf_op jit(solution)/shard_map/ppermute | solution.py:410
  4.5 13.4 %collective-permute-start.89 = (f32[584,128]{1,0:T(8,128)S(1)}, f32[584,128]{1,0:T(8,128)S(1)}, u32[]{:S(2)}, u32[]{:S(2)}) collective-permute-start(f32[584,128]{1,0:T(8,128)S(1)} %get-tuple-element.450), channel_id=1, source_target_pairs={{0,248},{1,249},{2,250},{3,251},{4,252},{5,253},{6,254},{7,255},{8... | collective-permute-start | bytes 897032 | tf_op jit(solution)/shard_map/ppermute | solution.py:411
  13.4 43.8 %collective-permute-start.90 = (f32[520,128]{1,0:T(8,128)S(1)}, f32[520,128]{1,0:T(8,128)S(1)}, u32[]{:S(2)}, u32[]{:S(2)}) collective-permute-start(f32[520,128]{1,0:T(8,128)S(1)} %get-tuple-element.451), channel_id=1, source_target_pairs={{0,1},{1,0},{2,3},{3,2},{4,5},{5,4},{6,7},{7,6},{8,9},{9,8},{10,11... | collective-permute-start | bytes 798728 | tf_op jit(solution)/shard_map/ppermute | solution.py:412
  16.1 41.1 %collective-permute-start.91 = (f32[520,128]{1,0:T(8,128)S(1)}, f32[520,128]{1,0:T(8,128)S(1)}, u32[]{:S(2)}, u32[]{:S(2)}) collective-permute-start(f32[520,128]{1,0:T(8,128)S(1)} %get-tuple-element.452), channel_id=1, source_target_pairs={{1,2},{2,1},{3,4},{4,3},{5,6},{6,5},{9,10},{10,9},{11,12},{12,11},... | collective-permute-start | bytes 798728 | tf_op jit(solution)/shard_map/ppermute | solution.py:413
  17.4 0.7 copy-start.7
  18.7 38.5 %copy-start.2 = (f32[1,3,2,8,128]{4,3,2,1,0:T(8,128)S(1)}, f32[1,3,2,8,128]{4,3,2,1,0:T(8,128)}, u32[]{:S(2)}) copy-start(f32[1,3,2,8,128]{4,3,2,1,0:T(8,128)} %param.68) | copy-start | bytes 73732
  18.7 38.5 %copy-start.3 = (f32[64,64]{1,0:T(8,128)S(1)}, f32[64,64]{1,0:T(8,128)}, u32[]{:S(2)}) copy-start(f32[64,64]{1,0:T(8,128)} %split_ref.3) | copy-start | bytes 49156
  18.8 38.5 %copy-start.4 = (f32[64,64]{1,0:T(8,128)S(1)}, f32[64,64]{1,0:T(8,128)}, u32[]{:S(2)}) copy-start(f32[64,64]{1,0:T(8,128)} %merge_ref.3) | copy-start | bytes 49156
  20.8 11.5 %collective-permute-start.23 = (f32[192,128]{1,0:T(8,128)S(1)}, f32[192,128]{1,0:T(8,128)S(1)}, u32[]{:S(2)}, u32[]{:S(2)}) collective-permute-start(f32[192,128]{1,0:T(8,128)S(1)} %get-tuple-element.333), channel_id=1, source_target_pairs={{7,263},{15,271},{23,279},{31,287},{39,295},{47,303},{55,311},{63,... | collective-permute-start | bytes 294920 | tf_op jit(solution)/shard_map/cond/branch_1_fun/cond/branch_0_fun/cond/branch_0_fun/cond/branch_0_fun/ppermute | solution.py:373
  23.5 31.7 %collective-permute-start.22 = (f32[320,128]{1,0:T(8,128)S(1)}, f32[320,128]{1,0:T(8,128)}, u32[]{:S(2)}, u32[]{:S(2)}) collective-permute-start(f32[320,128]{1,0:T(8,128)S(1)} %get-tuple-element.332), channel_id=1, source_target_pairs={{7,375},{15,383},{23,391},{31,399},{39,407},{47,415},{55,423},{63,... | collective-permute-start | bytes 491528 | tf_op jit(solution)/shard_map/cond/branch_1_fun/cond/branch_0_fun/cond/branch_0_fun/cond/branch_0_fun/ppermute | solution.py:374
  32.2 25.0 %collective-permute-start.24 = (f32[192,128]{1,0:T(8,128)S(1)}, f32[192,128]{1,0:T(8,128)}, u32[]{:S(2)}, u32[]{:S(2)}) collective-permute-start(f32[192,128]{1,0:T(8,128)S(1)} %collective-permute-done.23), channel_id=1, source_target_pairs={{7,151},{15,159},{23,167},{31,175},{39,183},{47,191},{55,199},{63,... | collective-permute-start | bytes 294920 | tf_op jit(solution)/shard_map/cond/branch_1_fun/cond/branch_0_fun/cond/branch_0_fun/cond/branch_0_fun/ppermute | solution.py:375
  57.2 0.7 copy-start.5
  60.2 7.4 %collective-permute-start.92 = (f32[576,128]{1,0:T(8,128)S(1)}, f32[576,128]{1,0:T(8,128)S(1)}, u32[]{:S(2)}, u32[]{:S(2)}) collective-permute-start(f32[576,128]{1,0:T(8,128)S(1)} %get-tuple-element.460), channel_id=1, source_target_pairs={{0,8},{1,9},{2,10},{3,11},{4,12},{5,13},{6,14},{7,15},{8,16},{9,17... | collective-permute-start | bytes 884744 | tf_op jit(solution)/shard_map/ppermute | solution.py:410
  60.3 7.3 %collective-permute-start.93 = (f32[576,128]{1,0:T(8,128)S(1)}, f32[576,128]{1,0:T(8,128)S(1)}, u32[]{:S(2)}, u32[]{:S(2)}) collective-permute-start(f32[576,128]{1,0:T(8,128)S(1)} %get-tuple-element.461), channel_id=1, source_target_pairs={{0,248},{1,249},{2,250},{3,251},{4,252},{5,253},{6,254},{7,255},{8... | collective-permute-start | bytes 884744 | tf_op jit(solution)/shard_map/ppermute | solution.py:411
  63.2 39.6 %collective-permute-start.94 = (f32[512,128]{1,0:T(8,128)}, f32[512,128]{1,0:T(8,128)S(1)}, u32[]{:S(2)}, u32[]{:S(2)}) collective-permute-start(f32[512,128]{1,0:T(8,128)} %get-tuple-element.462), channel_id=1, source_target_pairs={{0,1},{1,0},{2,3},{3,2},{4,5},{5,4},{6,7},{7,6},{8,9},{9,8},{10,11... | collective-permute-start | bytes 786440 | tf_op jit(solution)/shard_map/ppermute | solution.py:412
  65.1 37.7 %collective-permute-start.95 = (f32[512,128]{1,0:T(8,128)}, f32[512,128]{1,0:T(8,128)S(1)}, u32[]{:S(2)}, u32[]{:S(2)}) collective-permute-start(f32[512,128]{1,0:T(8,128)} %get-tuple-element.463), channel_id=1, source_target_pairs={{1,2},{2,1},{3,4},{4,3},{5,6},{6,5},{9,10},{10,9},{11,12},{12,11},... | collective-permute-start | bytes 786440 | tf_op jit(solution)/shard_map/ppermute | solution.py:413
  69.9 13.3 %collective-permute-start.73 = (f32[192,128]{1,0:T(8,128)S(1)}, f32[192,128]{1,0:T(8,128)S(1)}, u32[]{:S(2)}, u32[]{:S(2)}) collective-permute-start(f32[192,128]{1,0:T(8,128)S(1)} %get-tuple-element.402), channel_id=1, source_target_pairs={{7,263},{15,271},{23,279},{31,287},{39,295},{47,303},{55,311},{63,... | collective-permute-start | bytes 294920 | tf_op jit(solution)/shard_map/cond/branch_1_fun/cond/branch_0_fun/cond/branch_1_fun/cond/branch_0_fun/ppermute | solution.py:373
  72.8 30.0 %collective-permute-start.72 = (f32[320,128]{1,0:T(8,128)S(1)}, f32[320,128]{1,0:T(8,128)}, u32[]{:S(2)}, u32[]{:S(2)}) collective-permute-start(f32[320,128]{1,0:T(8,128)S(1)} %get-tuple-element.401), channel_id=1, source_target_pairs={{7,343},{15,351},{23,359},{31,367},{39,375},{47,383},{55,391},{63,... | collective-permute-start | bytes 491528 | tf_op jit(solution)/shard_map/cond/branch_1_fun/cond/branch_0_fun/cond/branch_1_fun/cond/branch_0_fun/ppermute | solution.py:374
  83.3 19.5 %collective-permute-start.74 = (f32[192,128]{1,0:T(8,128)S(1)}, f32[192,128]{1,0:T(8,128)}, u32[]{:S(2)}, u32[]{:S(2)}) collective-permute-start(f32[192,128]{1,0:T(8,128)S(1)} %collective-permute-done.73), channel_id=1, source_target_pairs={{7,183},{15,191},{23,199},{31,207},{39,215},{47,223},{55,231},{63,... | collective-permute-start | bytes 294920 | tf_op jit(solution)/shard_map/cond/branch_1_fun/cond/branch_0_fun/cond/branch_1_fun/cond/branch_0_fun/ppermute | solution.py:375

commit v3 on v2

--- a/solution.py
+++ b/solution.py
@@ -16,11 +16,9 @@
 AXIAL = 128
 ROW_BYTES_ROWS = CELLS * SECTIONS
 STRIDE = ROWS * CELLS
-PARTS = 4
-PART = SECTIONS // PARTS
 OWN = 40
 CROSS = SECTIONS - OWN
-DIRECT_CHIPS = 1
+DIRECT_CHIPS = 2
 EDGE = ROW_BYTES_ROWS + SECTIONS
 
 
@@ -72,42 +70,16 @@
 
 
 def pack_kernel(
-    shift_ref,
-    field_hbm,
-    speed_hbm,
-    low_ref,
-    high_ref,
-    first_block_ref,
-    second_block_ref,
-    next_ref,
-    prev_ref,
-    first_chips_ref,
-    second_chips_ref,
-    field_ref,
-    speed_ref,
-    sems,
+    field_ref, speed_ref, low_ref, high_ref, first_block_ref, second_block_ref, next_ref, prev_ref
 ):
-    copies = [pltpu.make_async_copy(speed_hbm, speed_ref, sems.at[PARTS])]
-    for part in range(PARTS):
-        where = pl.ds(part * PART * STRIDE, PART * STRIDE)
-        copies.append(pltpu.make_async_copy(field_hbm.at[where, :], field_ref.at[where, :], sems.at[part]))
-    for copy in copies:
-        copy.start()
-    for substep, chips_ref in enumerate((first_chips_ref, second_chips_ref)):
-        chips = (shift_ref[substep] + CELLS) // STRIDE % (lax.axis_size("sector") // 2)
-        chips_ref[...] = jnp.full((1, 1), chips, jnp.int32)
     up_is_first = is_even("block")
-    for part in range(PARTS):
-        copies[1 + part].wait()
-        for a in range(CELLS):
-            low, high = [
-                field_ref[pl.ds(part * PART * STRIDE + row * CELLS + a, PART, stride=STRIDE), :] for row in range(ROWS)
-            ]
-            store_cells(pl.ds(a * SECTIONS + part * PART, PART), low, high, up_is_first, low_ref, high_ref, first_block_ref, second_block_ref, next_ref, prev_ref)
-            if a in (0, CELLS - 1):
-                edge_ref = next_ref if a else prev_ref
-                edge_ref[pl.ds(ROW_BYTES_ROWS + part * PART, PART), :] = low
-    copies[0].wait()
+    for a in range(CELLS):
+        low, high = [field_ref[pl.ds(row * CELLS + a, SECTIONS, stride=STRIDE), :] for row in range(ROWS)]
+        store_cells(
+            line(a), low, high, up_is_first, low_ref, high_ref, first_block_ref, second_block_ref, next_ref, prev_ref
+        )
+        if a in (0, CELLS - 1):
+            (next_ref if a else prev_ref)[line(CELLS), :] = low
     low, high = [speed_ref[pl.ds(STRIDE + row * CELLS, CELLS), :] for row in range(ROWS)]
     first_block_ref[pl.ds(ROW_BYTES_ROWS, CELLS), :] = jnp.where(up_is_first, high, low)
     second_block_ref[pl.ds(ROW_BYTES_ROWS, CELLS), :] = jnp.where(up_is_first, low, high)
@@ -135,33 +107,27 @@
     return [pl.BlockSpec(memory_space=pltpu.VMEM)] * count
 
 
-def pack(shifts, field, speeds):
+def pack(field, speeds):
     row = lines(ROW_BYTES_ROWS)
     rim = lines(ROW_BYTES_ROWS + CELLS)
     edge = lines(EDGE + 8)
-    number = jax.ShapeDtypeStruct((1, 1), jnp.int32)
-    smem = pl.BlockSpec(memory_space=pltpu.SMEM)
     return pl.pallas_call(
         pack_kernel,
-        out_shape=(row, row, rim, rim, edge, edge, number, number),
-        in_specs=[smem] + [pl.BlockSpec(memory_space=pltpu.HBM)] * 2,
-        out_specs=tuple(vmem(8)),
-        scratch_shapes=[
-            pltpu.VMEM(field.shape, jnp.float32),
-            pltpu.VMEM(speeds.shape, jnp.float32),
-            pltpu.SemaphoreType.DMA((PARTS + 1,)),
-        ],
+        out_shape=(row, row, rim, rim, edge, edge),
+        in_specs=vmem(2),
+        out_specs=tuple(vmem(6)),
         compiler_params=pltpu.CompilerParams(vmem_limit_bytes=GRANT),
         name="pack",
-    )(shifts, field, speeds)
-
-
-def align_kernel(substep, shift_ref, weight_ref, own_ref, prev_ref, next_ref, direct_ref, cross_ref, row_ref):
+    )(field, speeds)
+
+
+def align_kernel(substep, shift_ref, weight_ref, own_ref, prev_ref, next_ref, _, direct_ref, cross_ref, row_ref):
     @pl.when(lax.axis_index("block") == lax.axis_size("block") - 1)
     def _():
         on_stator = lax.axis_index("region") == 1
-        residual = (shift_ref[substep] + CELLS) % STRIDE - CELLS
-        weight = weight_ref[substep]
+        chosen = lax.broadcasted_iota(jnp.int32, (1, 2), 1) == substep
+        residual = (jnp.sum(jnp.where(chosen, shift_ref[...], 0)) + CELLS) % STRIDE - CELLS
+        weight = jnp.sum(jnp.where(chosen, weight_ref[...], 0.0))
         for place, part_ref in enumerate((prev_ref, own_ref, next_ref)):
             row_ref[pl.ds(place * ROW_BYTES_ROWS, ROW_BYTES_ROWS), :] = part_ref[pl.ds(0, ROW_BYTES_ROWS), :]
         first = CELLS + jnp.where(on_stator, residual, -residual - 1)
@@ -176,16 +142,16 @@
             cross_ref[pl.ds(a * CROSS, CROSS), :] = ghost[OWN:]
 
 
-def align(substep, shifts, weights, own, from_prev, from_next):
+def align(substep, shifts, weights, own, from_prev, from_next, strain):
     return pl.pallas_call(
         functools.partial(align_kernel, substep),
         out_shape=(lines(CELLS * OWN), lines(CELLS * CROSS)),
-        in_specs=[pl.BlockSpec(memory_space=pltpu.SMEM)] * 2 + vmem(3),
+        in_specs=vmem(6),
         out_specs=tuple(vmem(2)),
         scratch_shapes=[pltpu.VMEM((3 * ROW_BYTES_ROWS, AXIAL), jnp.float32)],
         compiler_params=pltpu.CompilerParams(vmem_limit_bytes=GRANT),
         name="align",
-    )(shifts, weights, own, from_prev, from_next)
+    )(shifts, weights, own, from_prev, from_next, strain)
 
 
 def split_halves(value):
@@ -402,17 +368,19 @@
     field = number_concentration.reshape(SECTIONS * STRIDE, AXIAL)
     speeds = frame_motion_vector.reshape(3 * STRIDE, AXIAL)
     strain = strain_factor.reshape(STRIDE, AXIAL)
-    shifts, weights = spinning_shift_history, nearest_coverage_fraction
-    *arrays, first_chips, second_chips = pack(shifts, field, speeds)
+    shifts, weights = spinning_shift_history, nearest_coverage_fraction.reshape(1, 2)
+    arrays = pack(field, speeds)
     rims = None
-    for substep, chips in enumerate((first_chips, second_chips)):
+    chips = lax.rem(lax.div(shifts + CELLS, STRIDE), lax.axis_size("sector") // 2)
+    turns = lax.optimization_barrier((chips, lax.rev(chips, (0,))))
+    for substep in range(2):
         low, high, first, second, to_next, to_prev = arrays
         from_prev = lax.ppermute(to_next, AXES, sector_pairs(1))
         from_next = lax.ppermute(to_prev, AXES, sector_pairs(-1))
         first = lax.ppermute(first, AXES, block_pairs(0))
         second = lax.ppermute(second, AXES, block_pairs(1))
-        direct, cross = align(substep, shifts, weights, high, from_prev, from_next)
-        direct, cross = turned(chips[0, 0], direct, cross)
+        direct, cross = align(substep, shifts.reshape(1, 2), weights, high, from_prev, from_next, strain)
+        direct, cross = turned(turns[substep][0], direct, cross)
         halos = (from_prev, from_next, first, second)
         rims = rims or halos
         arrays = run_substep(

time: 106 us -> 84.6 us (0.80)
  the two profiles are of different devices: /device:TPU:30 before, /device:TPU:63 now
where the time goes in v3:
time: 84.6 us; the launch traced here: 84.2 us
  starting transfers between devices  38.2 us (45%)
  waiting for transfers between devices  37.9 us (45%)
  Pallas kernels  4.94 us (6%)
  local copies, waits for them, and re-layouts  2.55 us (3%)
    ppermute x2, waiting for transfers between devices, turn(): direct = lax.ppermute(direct, AXES, turn_pairs(2 * steps, True))  23.9 us
    ppermute x2, starting transfers between devices, turn(): direct = lax.ppermute(direct, AXES, turn_pairs(2 * steps, True))  16.7 us
    ppermute x1, waiting for transfers between devices, turn(): cross = lax.ppermute(cross, AXES, turn_pairs(2 * steps, True))  7.28 us
    ppermute x2, starting transfers between devices, body(): from_prev = lax.ppermute(to_next, AXES, sector_pairs(1))  5.37 us
    ppermute x2, waiting for transfers between devices, body(): from_next = lax.ppermute(to_prev, AXES, sector_pairs(-1))  5.25 us
    ppermute x1, starting transfers between devices, turn(): cross = lax.ppermute(cross, AXES, turn_pairs(0, True))  5.04 us
    pallas_call x2, Pallas kernels, run_substep(): pl.pallas_call(functools.partial(substep_kernel, final), out_shape=out_sh...  4.42 us
    ppermute x2, starting transfers between devices, body(): first = lax.ppermute(first, AXES, block_pairs(0))  4.4 us
  transfers between devices with their start and end apart: 13, of which 6 were waited for; matrix products, arithmetic and copies ran while one was open for 0% of the time, Pallas kernels for 0%

profile of v3, /device:TPU:63, one launch (start us, length us, event | category | flops | bytes accessed | tf_op | source)
XLA Modules:
  0.0 84.2 jit_solution(3975654295241419063)
XLA Ops:
  0.0 1.0 %copy-done = f32[1,64,2,8,128]{4,3,2,1,0:T(8,128)S(1)} copy-done((f32[1,64,2,8,128]{4,3,2,1,0:T(8,128)S(1)}, f32[1,64,2,8,128]{4,3,2,1,0:T(8,128)}, u32[]{:S(2)}) %copy-start) | copy-done | bytes 524312
  1.0 0.7 copy-done.1
  1.8 0.2 pack.1
  2.0 2.2 %collective-permute-start.84 = (f32[584,128]{1,0:T(8,128)S(1)}, f32[584,128]{1,0:T(8,128)S(1)}, u32[]{:S(2)}, u32[]{:S(2)}) collective-permute-start(f32[584,128]{1,0:T(8,128)S(1)} %get-tuple-element.449), channel_id=1, source_target_pairs={{0,8},{1,9},{2,10},{3,11},{4,12},{5,13},{6,14},{7,15},{8,16},{9,17... | collective-permute-start | bytes 897032 | tf_op jit(solution)/shard_map/ppermute | solution.py:378
  4.2 2.5 %collective-permute-start.86 = (f32[520,128]{1,0:T(8,128)S(1)}, f32[520,128]{1,0:T(8,128)S(1)}, u32[]{:S(2)}, u32[]{:S(2)}) collective-permute-start(f32[520,128]{1,0:T(8,128)S(1)} %get-tuple-element.451), channel_id=1, source_target_pairs={{0,1},{1,0},{2,3},{3,2},{4,5},{5,4},{6,7},{7,6},{8,9},{9,8},{10,11... | collective-permute-start | bytes 798728 | tf_op jit(solution)/shard_map/ppermute | solution.py:380
  6.7 0.7 collective-permute-start.87
  7.5 0.4 collective-permute-done.84.prev_ref.prev_rim_ref
  7.9 2.8 %collective-permute-done.85.next_ref.next_rim_ref = f32[584,128]{1,0:T(8,128)S(1)} collective-permute-done((f32[584,128]{1,0:T(8,128)S(1)}, f32[584,128]{1,0:T(8,128)S(1)}, u32[]{:S(2)}, u32[]{:S(2)}) %collective-permute-start.85) | collective-permute-done | bytes 299040 | tf_op jit(solution)/shard_map/ppermute | solution.py:379
  10.7 0.7 copy-done.7
  11.5 16.7 %conditional.30 = ((f32[320,128]{1,0:T(8,128)}, f32[192,128]{1,0:T(8,128)})) conditional(s32[]{:T(128)} %convert_element_type.90, (s32[]{:T(128)S(1)}, f32[320,128]{1,0:T(8,128)S(1)}, f32[192,128]{1,0:T(8,128)S(1)}) %tuple.287, (s32[]{:T(128)S(1)}, f32[320,128]{1,0:T(8,128)S(1)}, f32[192,128]{1,0:T(8,128)S(1)}) %tuple.288), branch_computations={%region_0.0_spmd, %region_15.0_spmd} | conditional | flops 6 | bytes 1441994 | solution.py:348
  11.6 16.6 %conditional.6 = ((f32[320,128]{1,0:T(8,128)}, f32[192,128]{1,0:T(8,128)})) conditional(s32[]{:T(128)} %convert_element_type.66, (s32[]{:T(128)S(1)}, f32[320,128]{1,0:T(8,128)S(1)}, f32[192,128]{1,0:T(8,128)S(1)}) %param.14, (s32[]{:T(128)S(1)}, f32[320,128]{1,0:T(8,128)S(1)}, f32[192,128]{1,0:T(8,128)S(1)}) %param.14), branch_computations={%region_1.0_spmd, %region_8.0_spmd} | conditional | flops 4 | bytes 1441980 | solution.py:348
  11.6 16.6 %conditional.2 = ((f32[320,128]{1,0:T(8,128)}, f32[192,128]{1,0:T(8,128)})) conditional(s32[]{:T(128)} %convert_element_type.62, (s32[]{:T(128)S(1)}, f32[320,128]{1,0:T(8,128)S(1)}, f32[192,128]{1,0:T(8,128)S(1)}) %param.6, (s32[]{:T(128)S(1)}, f32[320,128]{1,0:T(8,128)S(1)}, f32[192,128]{1,0:T(8,128)S(1)}) %param.6), branch_computations={%region_2.0_spmd, %region_5.0_spmd} | conditional | flops 2 | bytes 1441966 | solution.py:348
  11.7 16.5 %conditional = (f32[320,128]{1,0:T(8,128)}, f32[192,128]{1,0:T(8,128)}) conditional(s32[]{:T(128)} %convert_element_type.60, (f32[320,128]{1,0:T(8,128)S(1)}, f32[192,128]{1,0:T(8,128)S(1)}) %tuple.127, (f32[320,128]{1,0:T(8,128)S(1)}, f32[192,128]{1,0:T(8,128)S(1)}) %tuple.127), branch_computations={%region_3.0_spmd, %region_4.0_spmd} | conditional | bytes 1048672 | solution.py:348
  11.7 7.3 %collective-permute-start.2 = (f32[320,128]{1,0:T(8,128)S(1)}, f32[320,128]{1,0:T(8,128)}, u32[]{:S(2)}, u32[]{:S(2)}) collective-permute-start(f32[320,128]{1,0:T(8,128)S(1)} %get-tuple-element.303), channel_id=1, source_target_pairs={{7,487},{15,495},{23,503},{31,511},{39,263},{47,271},{55,279},{63,... | collective-permute-start | bytes 491528 | tf_op jit(solution)/shard_map/cond/branch_0_fun/cond/branch_0_fun/cond/branch_0_fun/cond/branch_1_fun/ppermute | solution.py:337
  19.0 1.9 %collective-permute-start.3 = (f32[192,128]{1,0:T(8,128)S(1)}, f32[192,128]{1,0:T(8,128)}, u32[]{:S(2)}, u32[]{:S(2)}) collective-permute-start(f32[192,128]{1,0:T(8,128)S(1)} %get-tuple-element.304), channel_id=1, source_target_pairs={{7,487},{15,495},{23,503},{31,511},{39,263},{47,271},{55,279},{63,... | collective-permute-start | bytes 294920 | tf_op jit(solution)/shard_map/cond/branch_0_fun/cond/branch_0_fun/cond/branch_0_fun/cond/branch_1_fun/ppermute | solution.py:336
  20.9 7.3 %collective-permute-done.3 = f32[192,128]{1,0:T(8,128)} collective-permute-done((f32[192,128]{1,0:T(8,128)S(1)}, f32[192,128]{1,0:T(8,128)}, u32[]{:S(2)}, u32[]{:S(2)}) %collective-permute-start.3) | collective-permute-done | bytes 98336 | tf_op jit(solution)/shard_map/cond/branch_0_fun/cond/branch_0_fun/cond/branch_0_fun/cond/branch_1_fun/ppermute | solution.py:336
  28.3 2.3 %substep.2 = (f32[512,128]{1,0:T(8,128)S(1)}, f32[512,128]{1,0:T(8,128)S(1)}, f32[512,128]{1,0:T(8,128)}, f32[512,128]{1,0:T(8,128)}, f32[576,128]{1,0:T(8,128)S(1)}, /*index=5*/f32[576,128]{1,0:T(8,128)S(1)}) custom-call(f32[512,128]{1,0:T(8,128)S(1)} %get-tuple-element.447.low_ref, f32[512,128]{1,0:T(8,128)S(1)} %get-tuple-element.448.own_ref.high_ref, ...), custom_call_target="tpu_custom_call" | custom-call | tf_op jit(solution)/shard_map/substep/pallas_call | solution.py:319
  30.5 3.2 %collective-permute-start.88 = (f32[576,128]{1,0:T(8,128)S(1)}, f32[576,128]{1,0:T(8,128)S(1)}, u32[]{:S(2)}, u32[]{:S(2)}) collective-permute-start(f32[576,128]{1,0:T(8,128)S(1)} %get-tuple-element.460), channel_id=1, source_target_pairs={{0,8},{1,9},{2,10},{3,11},{4,12},{5,13},{6,14},{7,15},{8,16},{9,17... | collective-permute-start | bytes 884744 | tf_op jit(solution)/shard_map/ppermute | solution.py:378
  33.7 1.9 %collective-permute-start.90 = (f32[512,128]{1,0:T(8,128)}, f32[512,128]{1,0:T(8,128)S(1)}, u32[]{:S(2)}, u32[]{:S(2)}) collective-permute-start(f32[512,128]{1,0:T(8,128)} %get-tuple-element.462), channel_id=1, source_target_pairs={{0,1},{1,0},{2,3},{3,2},{4,5},{5,4},{6,7},{7,6},{8,9},{9,8},{10,11... | collective-permute-start | bytes 786440 | tf_op jit(solution)/shard_map/ppermute | solution.py:380
  35.6 0.7 collective-permute-start.91
  36.3 1.0 %collective-permute-done.88.prev_ref = f32[576,128]{1,0:T(8,128)S(1)} collective-permute-done((f32[576,128]{1,0:T(8,128)S(1)}, f32[576,128]{1,0:T(8,128)S(1)}, u32[]{:S(2)}, u32[]{:S(2)}) %collective-permute-start.88) | collective-permute-done | bytes 294944 | tf_op jit(solution)/shard_map/ppermute | solution.py:378
  37.4 2.5 %collective-permute-done.89.next_ref = f32[576,128]{1,0:T(8,128)S(1)} collective-permute-done((f32[576,128]{1,0:T(8,128)S(1)}, f32[576,128]{1,0:T(8,128)S(1)}, u32[]{:S(2)}, u32[]{:S(2)}) %collective-permute-start.89) | collective-permute-done | bytes 294944 | tf_op jit(solution)/shard_map/ppermute | solution.py:379
  39.8 0.2 align.3
  40.0 42.0 %conditional.31 = ((f32[320,128]{1,0:T(8,128)}, f32[192,128]{1,0:T(8,128)})) conditional(s32[]{:T(128)} %convert_element_type.91, (s32[]{:T(128)S(1)}, f32[320,128]{1,0:T(8,128)S(1)}, f32[192,128]{1,0:T(8,128)S(1)}) %tuple.285, (s32[]{:T(128)S(1)}, f32[320,128]{1,0:T(8,128)S(1)}, f32[192,128]{1,0:T(8,128)S(1)}) %tuple.286), branch_computations={%region_30.0_spmd, %region_45.0_spmd} | conditional | flops 6 | bytes 1441994 | solution.py:348
  40.1 41.9 %conditional.20 = ((f32[320,128]{1,0:T(8,128)}, f32[192,128]{1,0:T(8,128)})) conditional(s32[]{:T(128)} %convert_element_type.80, (s32[]{:T(128)S(1)}, f32[320,128]{1,0:T(8,128)S(1)}, f32[192,128]{1,0:T(8,128)S(1)}) %param.44, (s32[]{:T(128)S(1)}, f32[320,128]{1,0:T(8,128)S(1)}, f32[192,128]{1,0:T(8,128)S(1)}) %param.44), branch_computations={%region_31.0_spmd, %region_38.0_spmd} | conditional | flops 4 | bytes 1441980 | solution.py:348
  40.1 41.9 %conditional.19 = ((f32[320,128]{1,0:T(8,128)}, f32[192,128]{1,0:T(8,128)})) conditional(s32[]{:T(128)} %convert_element_type.79, (s32[]{:T(128)S(1)}, f32[320,128]{1,0:T(8,128)S(1)}, f32[192,128]{1,0:T(8,128)S(1)}) %param.43, (s32[]{:T(128)S(1)}, f32[320,128]{1,0:T(8,128)S(1)}, f32[192,128]{1,0:T(8,128)S(1)}) %param.43), branch_computations={%region_39.0_spmd, %region_42.0_spmd} | conditional | flops 2 | bytes 1441966 | solution.py:348
  40.2 41.8 %conditional.18 = (f32[320,128]{1,0:T(8,128)}, f32[192,128]{1,0:T(8,128)}) conditional(s32[]{:T(128)} %convert_element_type.78, (f32[320,128]{1,0:T(8,128)S(1)}, f32[192,128]{1,0:T(8,128)S(1)}) %tuple.171, (f32[320,128]{1,0:T(8,128)S(1)}, f32[192,128]{1,0:T(8,128)S(1)}) %tuple.171), branch_computations={%region_43.0_spmd, %region_44.0_spmd} | conditional | bytes 1441928 | solution.py:348
  40.2 5.0 %collective-permute-start.59 = (f32[192,128]{1,0:T(8,128)S(1)}, f32[192,128]{1,0:T(8,128)S(1)}, u32[]{:S(2)}, u32[]{:S(2)}) collective-permute-start(f32[192,128]{1,0:T(8,128)S(1)} %get-tuple-element.386), channel_id=1, source_target_pairs={{7,263},{15,271},{23,279},{31,287},{39,295},{47,303},{55,311},{63,... | collective-permute-start | bytes 294920 | tf_op jit(solution)/shard_map/cond/branch_0_fun/cond/branch_1_fun/cond/branch_1_fun/cond/branch_0_fun/ppermute | solution.py:339
  45.2 9.4 %collective-permute-start.58 = (f32[320,128]{1,0:T(8,128)S(1)}, f32[320,128]{1,0:T(8,128)}, u32[]{:S(2)}, u32[]{:S(2)}) collective-permute-start(f32[320,128]{1,0:T(8,128)S(1)} %get-tuple-element.385), channel_id=1, source_target_pairs={{7,407},{15,415},{23,423},{31,431},{39,439},{47,447},{55,455},{63,... | collective-permute-start | bytes 491528 | tf_op jit(solution)/shard_map/cond/branch_0_fun/cond/branch_1_fun/cond/branch_1_fun/cond/branch_0_fun/ppermute | solution.py:340
  54.7 3.4 %collective-permute-start.60 = (f32[192,128]{1,0:T(8,128)S(1)}, f32[192,128]{1,0:T(8,128)}, u32[]{:S(2)}, u32[]{:S(2)}) collective-permute-start(f32[192,128]{1,0:T(8,128)S(1)} %collective-permute-done.59), channel_id=1, source_target_pairs={{7,119},{15,127},{23,135},{31,143},{39,151},{47,159},{55,167},{63,... | collective-permute-start | bytes 294920 | tf_op jit(solution)/shard_map/cond/branch_0_fun/cond/branch_1_fun/cond/branch_1_fun/cond/branch_0_fun/ppermute | solution.py:341
  58.1 23.9 %collective-permute-done.58 = f32[320,128]{1,0:T(8,128)} collective-permute-done((f32[320,128]{1,0:T(8,128)S(1)}, f32[320,128]{1,0:T(8,128)}, u32[]{:S(2)}, u32[]{:S(2)}) %collective-permute-start.58) | collective-permute-done | bytes 163872 | tf_op jit(solution)/shard_map/cond/branch_0_fun/cond/branch_1_fun/cond/branch_1_fun/cond/branch_0_fun/ppermute | solution.py:340
  82.0 2.1 %substep.3 = f32[64,16,128]{2,1,0:T(8,128)} custom-call(f32[512,128]{1,0:T(8,128)S(1)} %get-tuple-element.458.low_ref, f32[512,128]{1,0:T(8,128)S(1)} %get-tuple-element.459.own_ref.high_ref, f32[576,128]{1,0:T(8,128)S(1)} %collective-permute-done.88.prev_ref, f32[576,128]{1,0:T(8,128)S(1)} %collective-permute-done.89.next_ref, ...), custom_call_target="tpu_custom_call" | custom-call | tf_op jit(solution)/shard_map/substep/pallas_call | solution.py:319
  (25 shorter events, 0.3 us)
Async XLA Ops:
  0.0 1.0 %copy-start = (f32[1,64,2,8,128]{4,3,2,1,0:T(8,128)S(1)}, f32[1,64,2,8,128]{4,3,2,1,0:T(8,128)}, u32[]{:S(2)}) copy-start(f32[1,64,2,8,128]{4,3,2,1,0:T(8,128)} %param.67) | copy-start | bytes 1572868
  1.0 0.7 copy-start.1
  2.0 5.9 %collective-permute-start.84 = (f32[584,128]{1,0:T(8,128)S(1)}, f32[584,128]{1,0:T(8,128)S(1)}, u32[]{:S(2)}, u32[]{:S(2)}) collective-permute-start(f32[584,128]{1,0:T(8,128)S(1)} %get-tuple-element.449), channel_id=1, source_target_pairs={{0,8},{1,9},{2,10},{3,11},{4,12},{5,13},{6,14},{7,15},{8,16},{9,17... | collective-permute-start | bytes 897032 | tf_op jit(solution)/shard_map/ppermute | solution.py:378
  4.2 6.5 %collective-permute-start.85 = (f32[584,128]{1,0:T(8,128)S(1)}, f32[584,128]{1,0:T(8,128)S(1)}, u32[]{:S(2)}, u32[]{:S(2)}) collective-permute-start(f32[584,128]{1,0:T(8,128)S(1)} %get-tuple-element.450), channel_id=1, source_target_pairs={{0,248},{1,249},{2,250},{3,251},{4,252},{5,253},{6,254},{7,255},{8... | collective-permute-start | bytes 897032 | tf_op jit(solution)/shard_map/ppermute | solution.py:379
  4.2 3.2 %copy-start.6 = (s32[2]{0:T(128)S(1)}, s32[2]{0:T(128)}, u32[]{:S(2)}) copy-start(s32[2]{0:T(128)} %param.72) | copy-start | bytes 28
  4.2 24.0 %collective-permute-start.86 = (f32[520,128]{1,0:T(8,128)S(1)}, f32[520,128]{1,0:T(8,128)S(1)}, u32[]{:S(2)}, u32[]{:S(2)}) collective-permute-start(f32[520,128]{1,0:T(8,128)S(1)} %get-tuple-element.451), channel_id=1, source_target_pairs={{0,1},{1,0},{2,3},{3,2},{4,5},{5,4},{6,7},{7,6},{8,9},{9,8},{10,11... | collective-permute-start | bytes 798728 | tf_op jit(solution)/shard_map/ppermute | solution.py:380
  6.7 21.5 %collective-permute-start.87 = (f32[520,128]{1,0:T(8,128)S(1)}, f32[520,128]{1,0:T(8,128)S(1)}, u32[]{:S(2)}, u32[]{:S(2)}) collective-permute-start(f32[520,128]{1,0:T(8,128)S(1)} %get-tuple-element.452), channel_id=1, source_target_pairs={{1,2},{2,1},{3,4},{4,3},{5,6},{6,5},{9,10},{10,9},{11,12},{12,11},... | collective-permute-start | bytes 798728 | tf_op jit(solution)/shard_map/ppermute | solution.py:381
  7.5 3.2 %copy-start.5 = (f32[1,2,8,128]{3,2,1,0:T(8,128)S(1)}, f32[1,2,8,128]{3,2,1,0:T(8,128)}, u32[]{:S(2)}) copy-start(f32[1,2,8,128]{3,2,1,0:T(8,128)} %param.69) | copy-start | bytes 24580
  10.7 0.7 copy-start.7
  11.5 16.7 %copy-start.2 = (f32[1,3,2,8,128]{4,3,2,1,0:T(8,128)S(1)}, f32[1,3,2,8,128]{4,3,2,1,0:T(8,128)}, u32[]{:S(2)}) copy-start(f32[1,3,2,8,128]{4,3,2,1,0:T(8,128)} %param.68) | copy-start | bytes 73732
  11.5 16.7 %copy-start.3 = (f32[64,64]{1,0:T(8,128)S(1)}, f32[64,64]{1,0:T(8,128)}, u32[]{:S(2)}) copy-start(f32[64,64]{1,0:T(8,128)} %split_ref.3) | copy-start | bytes 49156
  11.5 16.7 %copy-start.4 = (f32[64,64]{1,0:T(8,128)S(1)}, f32[64,64]{1,0:T(8,128)}, u32[]{:S(2)}) copy-start(f32[64,64]{1,0:T(8,128)} %merge_ref.3) | copy-start | bytes 49156
  11.7 16.5 %collective-permute-start.2 = (f32[320,128]{1,0:T(8,128)S(1)}, f32[320,128]{1,0:T(8,128)}, u32[]{:S(2)}, u32[]{:S(2)}) collective-permute-start(f32[320,128]{1,0:T(8,128)S(1)} %get-tuple-element.303), channel_id=1, source_target_pairs={{7,487},{15,495},{23,503},{31,511},{39,263},{47,271},{55,279},{63,... | collective-permute-start | bytes 491528 | tf_op jit(solution)/shard_map/cond/branch_0_fun/cond/branch_0_fun/cond/branch_0_fun/cond/branch_1_fun/ppermute | solution.py:337
  19.0 9.2 %collective-permute-start.3 = (f32[192,128]{1,0:T(8,128)S(1)}, f32[192,128]{1,0:T(8,128)}, u32[]{:S(2)}, u32[]{:S(2)}) collective-permute-start(f32[192,128]{1,0:T(8,128)S(1)} %get-tuple-element.304), channel_id=1, source_target_pairs={{7,487},{15,495},{23,503},{31,511},{39,263},{47,271},{55,279},{63,... | collective-permute-start | bytes 294920 | tf_op jit(solution)/shard_map/cond/branch_0_fun/cond/branch_0_fun/cond/branch_0_fun/cond/branch_1_fun/ppermute | solution.py:336
  30.5 6.8 %collective-permute-start.88 = (f32[576,128]{1,0:T(8,128)S(1)}, f32[576,128]{1,0:T(8,128)S(1)}, u32[]{:S(2)}, u32[]{:S(2)}) collective-permute-start(f32[576,128]{1,0:T(8,128)S(1)} %get-tuple-element.460), channel_id=1, source_target_pairs={{0,8},{1,9},{2,10},{3,11},{4,12},{5,13},{6,14},{7,15},{8,16},{9,17... | collective-permute-start | bytes 884744 | tf_op jit(solution)/shard_map/ppermute | solution.py:378
  33.7 6.1 %collective-permute-start.89 = (f32[576,128]{1,0:T(8,128)S(1)}, f32[576,128]{1,0:T(8,128)S(1)}, u32[]{:S(2)}, u32[]{:S(2)}) collective-permute-start(f32[576,128]{1,0:T(8,128)S(1)} %get-tuple-element.461), channel_id=1, source_target_pairs={{0,248},{1,249},{2,250},{3,251},{4,252},{5,253},{6,254},{7,255},{8... | collective-permute-start | bytes 884744 | tf_op jit(solution)/shard_map/ppermute | solution.py:379
  33.7 48.3 %collective-permute-start.90 = (f32[512,128]{1,0:T(8,128)}, f32[512,128]{1,0:T(8,128)S(1)}, u32[]{:S(2)}, u32[]{:S(2)}) collective-permute-start(f32[512,128]{1,0:T(8,128)} %get-tuple-element.462), channel_id=1, source_target_pairs={{0,1},{1,0},{2,3},{3,2},{4,5},{5,4},{6,7},{7,6},{8,9},{9,8},{10,11... | collective-permute-start | bytes 786440 | tf_op jit(solution)/shard_map/ppermute | solution.py:380
  35.6 46.4 %collective-permute-start.91 = (f32[512,128]{1,0:T(8,128)}, f32[512,128]{1,0:T(8,128)S(1)}, u32[]{:S(2)}, u32[]{:S(2)}) collective-permute-start(f32[512,128]{1,0:T(8,128)} %get-tuple-element.463), channel_id=1, source_target_pairs={{1,2},{2,1},{3,4},{4,3},{5,6},{6,5},{9,10},{10,9},{11,12},{12,11},... | collective-permute-start | bytes 786440 | tf_op jit(solution)/shard_map/ppermute | solution.py:381
  40.2 14.5 %collective-permute-start.59 = (f32[192,128]{1,0:T(8,128)S(1)}, f32[192,128]{1,0:T(8,128)S(1)}, u32[]{:S(2)}, u32[]{:S(2)}) collective-permute-start(f32[192,128]{1,0:T(8,128)S(1)} %get-tuple-element.386), channel_id=1, source_target_pairs={{7,263},{15,271},{23,279},{31,287},{39,295},{47,303},{55,311},{63,... | collective-permute-start | bytes 294920 | tf_op jit(solution)/shard_map/cond/branch_0_fun/cond/branch_1_fun/cond/branch_1_fun/cond/branch_0_fun/ppermute | solution.py:339
  45.2 36.8 %collective-permute-start.58 = (f32[320,128]{1,0:T(8,128)S(1)}, f32[320,128]{1,0:T(8,128)}, u32[]{:S(2)}, u32[]{:S(2)}) collective-permute-start(f32[320,128]{1,0:T(8,128)S(1)} %get-tuple-element.385), channel_id=1, source_target_pairs={{7,407},{15,415},{23,423},{31,431},{39,439},{47,447},{55,455},{63,... | collective-permute-start | bytes 491528 | tf_op jit(solution)/shard_map/cond/branch_0_fun/cond/branch_1_fun/cond/branch_1_fun/cond/branch_0_fun/ppermute | solution.py:340
  54.7 27.3 %collective-permute-start.60 = (f32[192,128]{1,0:T(8,128)S(1)}, f32[192,128]{1,0:T(8,128)}, u32[]{:S(2)}, u32[]{:S(2)}) collective-permute-start(f32[192,128]{1,0:T(8,128)S(1)} %collective-permute-done.59), channel_id=1, source_target_pairs={{7,119},{15,127},{23,135},{31,143},{39,151},{47,159},{55,167},{63,... | collective-permute-start | bytes 294920 | tf_op jit(solution)/shard_map/cond/branch_0_fun/cond/branch_1_fun/cond/branch_1_fun/cond/branch_0_fun/ppermute | solution.py:341
